TPU v7x, 256 devices: a whole 4x4x8 slice. The times are simulated.
256 devices in a mesh: row: 32 (over y, x, core), col: 8 (over z).
Axes of the slice: x: 4, y: 4, z: 8, core: 2. Of those that a mesh axis runs over, the one named last changes fastest.
Arguments:
- sigma_anc: bfloat16 [40, 256, 10240], P('col', 'row'), as said below
- lower_off: bfloat16 [8192, 4096], P('row', 'col'), may hold values from -0.01171875 to 0.01171875
- inverse_diag: bfloat16 [4096, 4096], P('row', 'col'), as said below
- structure: int32 [32], replicated, may hold values from 0 to 39, as said below
Outputs:
- sigma_off: bfloat16 [8192, 4096], P('row', 'col')
- sigma_front: float32 [4096, 4096], P('row', 'col')
Inputs may be any that keep to these rules, and one draw needn't show every extreme that they name: `structure`: strictly increasing ancestor block indices. `sigma_anc`: exactly symmetric when read as a 10240 x 10240 matrix. `inverse_diag`: zero above the diagonal.
All inputs are finite; a program needn't handle non-finite values.
Results may differ from a plain program's by a relative error of at most 0.005.
Values may be sent and summed in bfloat16 or wider, within the bound.
A program may use at most 64 MiB of HBM per device.

v0:
```python
import jax
import jax.numpy as jnp
from jax import lax
from jax.sharding import PartitionSpec as P


def contract_rows(left, right):
    flipped = lax.optimization_barrier(jnp.transpose(left))
    return jnp.dot(flipped, right, preferred_element_type=jnp.float32)


def per_device(sigma_anc, lower_off, inverse_diag, structure):
    n_col = lax.axis_size("col")
    col_pos = lax.axis_index("col")
    blocks_here, sub_rows, anc_width = sigma_anc.shape
    block = anc_width // (blocks_here * n_col)
    count = structure.shape[0]
    per_col = count // n_col
    width = count * block
    picked = jnp.take(
        sigma_anc.reshape(blocks_here, sub_rows, anc_width // block, block), structure, axis=2
    )
    picked = picked.reshape(blocks_here, sub_rows, width)
    placing = jnp.transpose(structure.reshape(per_col, n_col))
    local_ids = placing - col_pos * blocks_here
    present = (local_ids >= 0) & (local_ids < blocks_here)
    safe_ids = jnp.clip(local_ids, 0, blocks_here - 1).reshape(-1)
    outgoing = jnp.take(picked, safe_ids, axis=0).reshape(n_col, per_col, sub_rows, width)
    outgoing = jnp.where(present[:, :, None, None], outgoing, jnp.zeros_like(outgoing))
    incoming = lax.all_to_all(outgoing, "col", split_axis=0, concat_axis=0, tiled=True)
    mine = jnp.take(placing, col_pos, axis=0)
    sender = mine // blocks_here
    own_rows = incoming[sender, jnp.arange(per_col, dtype=jnp.int32)]
    restriped = lax.all_to_all(own_rows, "row", split_axis=2, concat_axis=1, tiled=True)
    gathered = lax.all_gather(restriped, "col", axis=0, tiled=True)
    strip = jnp.transpose(gathered.reshape(n_col, per_col, block, block), (3, 1, 0, 2)).reshape(
        block, width
    )
    lower_strip = lax.all_gather(lower_off, "col", axis=1, tiled=True)
    inverse_all = lax.all_gather(inverse_diag, "row", axis=0, tiled=True)
    upper = jnp.dot(lower_strip, inverse_all, preferred_element_type=jnp.float32).astype(
        jnp.bfloat16
    )
    upper_all = lax.all_gather(upper, "row", axis=0, tiled=True)
    sigma_off = (-jnp.dot(strip, upper_all, preferred_element_type=jnp.float32)).astype(
        jnp.bfloat16
    )
    sigma_rows, inverse_rows = (
        lax.all_gather(sigma_off, "col", axis=1, tiled=True),
        lax.all_gather(inverse_diag, "col", axis=1, tiled=True),
    )
    sigma_cols, inverse_cols_part = (
        lax.all_to_all(sigma_rows, "row", split_axis=1, concat_axis=0, tiled=True),
        lax.all_to_all(inverse_rows, "row", split_axis=1, concat_axis=0, tiled=True),
    )
    sigma_front = contract_rows(inverse_cols_part, inverse_all) - contract_rows(
        sigma_cols, upper_all
    )
    return (sigma_off, sigma_front)


def solution(mesh):
    in_specs = (P("col", "row", None), P("row", "col"), P("row", "col"), P())
    out_specs = (P("row", "col"), P("row", "col"))
    return jax.shard_map(
        per_device, mesh=mesh, in_specs=in_specs, out_specs=out_specs, check_vma=False
    )
```

profile of v0, /device:TPU:24, one launch (start us, length us, event | category | flops | bytes accessed | tf_op | source)
XLA Modules:
  0.0 444.6 jit_solution(1136679891026021203)
XLA Ops:
  7.2 0.7 all-gather.9.cloned.1.call-update
  8.0 0.7 all-gather.11.cloned.1.call-update
  8.7 0.7 reshape.125
  9.4 0.7 compare_select_fusion.3
  10.1 0.7 compare_and_fusion
  11.0 0.6 gather_fusion
  12.0 2.8 gather_fusion.1
  14.9 4.7 %select_select_fusion = bf16[8,4,8,8192]{3,2,1,0:T(8,128)(2,1)} fusion(bf16[8,4,8,8192]{3,2,1,0:T(8,128)(2,1)} %bitcast.49, pred[8,4]{1,0:T(8,128)(4,1)S(1)} %copy.31, pred[8,4]{1,0:T(8,128)(4,1)S(1)} %copy.30), kind=kLoop, calls=%fused_computation.3 | loop fusion | flops 4194304 | bytes 8388672 | tf_op jit(solution)/shard_map/jit(_where)/select_n | solution.py:29
  19.5 8.5 %all-to-all-start = ((bf16[8,4,8,8192]{3,2,1,0:T(8,128)(2,1)}), bf16[8,4,8,8192]{3,2,1,0:T(8,128)(2,1)}, u32[]{:S(2)}, u32[]{:S(2)}) async-start(bf16[8,4,8,8192]{3,2,1,0:T(8,128)(2,1)} %select_select_fusion), calls=%async_computation | async-start | bytes 8388608 | tf_op jit(solution)/shard_map/all_to_all | solution.py:30
  28.3 108.2 %all-to-all-done = bf16[8,4,8,8192]{3,2,1,0:T(8,128)(2,1)} async-done(((bf16[8,4,8,8192]{3,2,1,0:T(8,128)(2,1)}), bf16[8,4,8,8192]{3,2,1,0:T(8,128)(2,1)}, u32[]{:S(2)}, u32[]{:S(2)}) %all-to-all-start) | async-done | bytes 4194336 | tf_op jit(solution)/shard_map/all_to_all | solution.py:30
  136.5 2.9 gather_fusion.2
  139.4 8.2 %copy.34 = bf16[4,8,8192]{1,0,2:T(4,128)(2,1)} copy(bf16[4,8,8192]{2,1,0:T(8,128)(2,1)S(1)} %gather_fusion.2) | data formatting | bytes 1048576 | tf_op jit(solution)/shard_map/gather | solution.py:33
  147.7 10.5 %reshape.212 = bf16[32,2,4096]{2,1,0:T(2,128)(2,1)S(1)} reshape(bf16[8192,4,8]{2,1,0:T(4,128)(2,1)} %bitcast.46) | data formatting | bytes 1048576
  158.1 17.3 %all_to_all.61 = bf16[32,2,4096]{2,1,0:T(2,128)(2,1)S(1)} all-to-all(bf16[32,2,4096]{2,1,0:T(2,128)(2,1)S(1)} %reshape.212), channel_id=1, replica_groups=mesh['row'=32,'col'=8] {'row'}, dimensions={0} | all-to-all | bytes 1048576 | tf_op jit(solution)/shard_map/all_to_all | solution.py:34
  175.4 11.0 %reshape.213 = bf16[8192,4,8]{2,1,0:T(4,128)(2,1)} reshape(bf16[32,2,4096]{2,1,0:T(2,128)(2,1)S(1)} %all_to_all.61) | data formatting | bytes 1048576
  186.4 11.0 %copy.35 = bf16[4,32,8,256]{3,2,1,0:T(8,128)(2,1)} copy(bf16[4,32,8,256]{2,0,3,1:T(4,128)(2,1)} %bitcast.47) | data formatting | bytes 1048576 | tf_op jit(solution)/shard_map/all_to_all | solution.py:34
  197.5 4.8 %convolution_convert_fusion = bf16[256,512]{1,0:T(8,128)(2,1)} fusion(bf16[256,4096]{1,0:T(8,128)(2,1)} %all-gather.9.cloned.1.call-done, bf16[4096,512]{1,0:T(8,128)(2,1)} %all-gather.11.cloned.1.call-done), kind=kOutput, calls=%fused_computation.6 | convolution fusion | flops 1073872896 | bytes 6553600 | tf_op jit(solution)/shard_map/dot_general | solution.py:41
  202.4 0.8 copy.37
  203.2 47.5 %all-gather.7.cloned.1.call-done = bf16[32,256,256]{2,1,0:T(8,128)(2,1)} async-done(((bf16[4,256,256]{2,1,0:T(8,128)(2,1)}), bf16[32,256,256]{2,1,0:T(8,128)(2,1)}) %all-gather.7.cloned.1.call-update) | async-done | bytes 4194320 | tf_op jit(solution)/shard_map/all_gather | solution.py:35
  250.7 4.6 %copy.36 = bf16[256,4,8,256]{0,3,2,1:T(8,128)(2,1)} copy(bf16[256,4,8,256]{0,3,1,2:T(8,128)(2,1)} %bitcast.51) | data formatting | bytes 8388608 | tf_op jit(solution)/shard_map/transpose | solution.py:36
  255.3 54.7 %all-gather.13.cloned.1.call-done = bf16[8192,512]{1,0:T(8,128)(2,1)} async-done(((bf16[256,512]{1,0:T(8,128)(2,1)}), bf16[8192,512]{1,0:T(8,128)(2,1)}) %all-gather.13.cloned.1.call-update) | async-done | bytes 8388624 | tf_op jit(solution)/shard_map/all_gather | solution.py:44
  310.0 7.7 %fusion = bf16[256,512]{1,0:T(8,128)(2,1)} fusion(bf16[256,8192]{0,1:T(8,128)(2,1)} %bitcast.48, bf16[8192,512]{1,0:T(8,128)(2,1)} %all-gather.13.cloned.1.call-done), kind=kOutput, calls=%fused_computation.7 | convolution fusion | flops 2147745792 | bytes 12845056 | tf_op jit(solution)/shard_map/dot_general | solution.py:45
  317.7 32.5 %all-gather.15.cloned.1.call-done = bf16[128,4096]{0,1:T(8,128)(2,1)} async-done(((bf16[128,512]{0,1:T(8,128)(2,1)}), bf16[128,4096]{0,1:T(8,128)(2,1)}) %all-gather.15.cloned.1.call-update) | async-done | bytes 1048592 | tf_op jit(solution)/shard_map/all_gather | solution.py:50
  350.3 7.4 %all-to-all-start.2 = ((bf16[128,32,128]{0,2,1:T(8,128)(2,1)}), bf16[128,32,128]{0,2,1:T(8,128)(2,1)S(1)}, u32[]{:S(2)}, u32[]{:S(2)}) async-start(bf16[128,32,128]{0,2,1:T(8,128)(2,1)} %bitcast.57), calls=%async_computation.2 | async-start | bytes 2097152 | tf_op jit(solution)/shard_map/all_to_all | solution.py:54
  357.7 34.7 %all-gather.17.cloned.1.call-done = bf16[256,4096]{1,0:T(8,128)(2,1)} async-done(((bf16[256,512]{1,0:T(8,128)(2,1)}), bf16[256,4096]{1,0:T(8,128)(2,1)}) %all-gather.17.cloned.1.call-update) | async-done | bytes 2097168 | tf_op jit(solution)/shard_map/all_gather | solution.py:49
  392.4 3.5 copy_bitcast_fusion
  395.8 1.0 copy-done.3
  396.8 7.4 %all-to-all-start.3 = ((bf16[256,32,128]{2,0,1:T(8,128)(2,1)}), bf16[256,32,128]{2,0,1:T(8,128)(2,1)S(1)}, u32[]{:S(2)}, u32[]{:S(2)}) async-start(bf16[256,32,128]{2,0,1:T(8,128)(2,1)} %copy_bitcast_fusion), calls=%async_computation.3 | async-start | bytes 4194304 | tf_op jit(solution)/shard_map/all_to_all | solution.py:53
  404.2 2.3 copy.38
  406.5 25.0 %all-to-all-done.3 = bf16[256,32,128]{2,0,1:T(8,128)(2,1)S(1)} async-done(((bf16[256,32,128]{2,0,1:T(8,128)(2,1)}), bf16[256,32,128]{2,0,1:T(8,128)(2,1)S(1)}, u32[]{:S(2)}, u32[]{:S(2)}) %all-to-all-start.3) | async-done | bytes 2097184 | tf_op jit(solution)/shard_map/all_to_all | solution.py:53
  431.5 4.8 %fusion.7 = f32[128,512]{1,0:T(8,128)S(1)} fusion(bf16[128,8192]{0,1:T(8,128)(2,1)S(1)} %bitcast.50, bf16[8192,512]{1,0:T(8,128)(2,1)} %all-gather.13.cloned.1.call-done), kind=kOutput, calls=%fused_computation.30 | convolution fusion | flops 1073741824 | bytes 10747904 | tf_op jit(solution)/shard_map/dot_general | solution.py:9
  436.3 1.5 convolution_subtract_fusion
  (38 shorter events, 1.2 us)
Async XLA Ops:
  7.2 3.8 copy-start
  7.2 190.3 %all-gather.9.cloned.1.call-start = ((), (), s32[]{:S(2)}) async-start(), calls=%async_computation.5 | async-start | bytes 2359296 | tf_op jit(solution)/shard_map/all_gather | solution.py:39
  7.9 189.6 %all-gather.11.cloned.1.call-start = ((), (), s32[]{:S(2)}) async-start(), calls=%async_computation.6 | async-start | bytes 4325376 | tf_op jit(solution)/shard_map/all_gather | solution.py:40
  19.5 116.9 %all-to-all-start = ((bf16[8,4,8,8192]{3,2,1,0:T(8,128)(2,1)}), bf16[8,4,8,8192]{3,2,1,0:T(8,128)(2,1)}, u32[]{:S(2)}, u32[]{:S(2)}) async-start(bf16[8,4,8,8192]{3,2,1,0:T(8,128)(2,1)} %select_select_fusion), calls=%async_computation | async-start | bytes 8388608 | tf_op jit(solution)/shard_map/all_to_all | solution.py:30
  28.0 222.7 %all-gather.7.cloned.1.call-start = ((), (), s32[]{:S(2)}) async-start(), calls=%async_computation.4 | async-start | bytes 4718592 | tf_op jit(solution)/shard_map/all_gather | solution.py:35
  197.4 5.0 %copy-start.5 = (bf16[128,512]{1,0:T(8,128)(2,1)S(1)}, bf16[128,512]{1,0:T(8,128)(2,1)}, u32[]{:S(2)}) copy-start(bf16[128,512]{1,0:T(8,128)(2,1)} %param.6) | copy-start | bytes 393220
  197.4 112.6 %all-gather.13.cloned.1.call-start = ((), (), s32[]{:S(2)}) async-start(), calls=%async_computation.7 | async-start | bytes 8650752 | tf_op jit(solution)/shard_map/all_gather | solution.py:44
  202.3 147.9 %all-gather.15.cloned.1.call-start = ((), (), s32[]{:S(2)}) async-start(), calls=%async_computation.8 | async-start | bytes 1179648 | tf_op jit(solution)/shard_map/all_gather | solution.py:50
  203.2 189.2 %all-gather.17.cloned.1.call-start = ((), (), s32[]{:S(2)}) async-start(), calls=%async_computation.9 | async-start | bytes 2359296 | tf_op jit(solution)/shard_map/all_gather | solution.py:49
  350.3 45.6 %all-to-all-start.2 = ((bf16[128,32,128]{0,2,1:T(8,128)(2,1)}), bf16[128,32,128]{0,2,1:T(8,128)(2,1)S(1)}, u32[]{:S(2)}, u32[]{:S(2)}) async-start(bf16[128,32,128]{0,2,1:T(8,128)(2,1)} %bitcast.57), calls=%async_computation.2 | async-start | bytes 2097152 | tf_op jit(solution)/shard_map/all_to_all | solution.py:54
  395.8 1.0 copy-start.3
  396.8 34.6 %all-to-all-start.3 = ((bf16[256,32,128]{2,0,1:T(8,128)(2,1)}), bf16[256,32,128]{2,0,1:T(8,128)(2,1)S(1)}, u32[]{:S(2)}, u32[]{:S(2)}) async-start(bf16[256,32,128]{2,0,1:T(8,128)(2,1)} %copy_bitcast_fusion), calls=%async_computation.3 | async-start | bytes 4194304 | tf_op jit(solution)/shard_map/all_to_all | solution.py:53
  431.5 4.8 %copy-start.2 = (bf16[4096,512]{1,0:T(8,128)(2,1)S(1)}, bf16[4096,512]{1,0:T(8,128)(2,1)}, u32[]{:S(2)}) copy-start(bf16[4096,512]{1,0:T(8,128)(2,1)} %all-gather.11.cloned.1.call-done) | copy-start | bytes 12582916
  431.5 4.9 %copy-start.4 = (bf16[32,128,128]{2,1,0:T(8,128)(2,1)S(1)}, bf16[32,128,128]{2,1,0:T(8,128)(2,1)}, u32[]{:S(2)}) copy-start(bf16[32,128,128]{2,1,0:T(8,128)(2,1)} %copy.38) | copy-start | bytes 3145732
  431.5 6.3 %copy-start.1 = (bf16[5,8,10240]{2,1,0:T(8,128)(2,1)S(1)}, bf16[5,8,10240]{2,1,0:T(8,128)(2,1)}, u32[]{:S(2)}) copy-start(bf16[5,8,10240]{2,1,0:T(8,128)(2,1)} %param.4) | copy-start | bytes 2457604
Sparse Core Ops, SparseCore 0:
  9.8 82.4 all-gather.8
  94.8 53.0 all-gather.10
  197.6 53.1 all-gather.6
  253.7 56.2 all-gather.12
  311.6 38.5 all-gather.14
  352.5 39.8 all-gather.16
where the time goes:
time: 447 us; the launch traced here: 445 us
  waiting for transfers between devices  304 us (68%)
  local copies, waits for them, and re-layouts  60.5 us (14%)
  starting transfers between devices  23.5 us (5%)
  matrix products  18.8 us (4%)
  blocking collectives  17.3 us (4%)
  between operations  14.3 us (3%)
  other arithmetic  6.31 us (1%)
    all_to_all x1, waiting for transfers between devices, per_device(): lax.all_to_all(outgoing, 'col', split_axis=0, concat_axis=0, tiled=True)  108 us
    all_gather x1, waiting for transfers between devices, per_device(): upper_all = lax.all_gather(upper, 'row', axis=0, tiled=True)  54.7 us
    all_gather x1, waiting for transfers between devices, per_device(): gathered = lax.all_gather(restriped, 'col', axis=0, tiled=True)  47.5 us
    all_gather x1, waiting for transfers between devices, per_device(): lax.all_gather(sigma_off, 'col', axis=1, tiled=True)  34.7 us
    all_gather x1, waiting for transfers between devices, per_device(): lax.all_gather(inverse_diag, 'col', axis=1, tiled=True)  32.5 us
    all_to_all x1, waiting for transfers between devices, per_device(): lax.all_to_all(sigma_rows, 'row', split_axis=1, concat_axis=0, tiled=True)  25 us
    unnamed x15, local copies, waits for them, and re-layouts  23.3 us
    all_to_all x1, blocking collectives, per_device(): lax.all_to_all(own_rows, 'row', split_axis=2, concat_axis=1, tiled=True)  17.3 us
  transfers between devices with their start and end apart: 9, of which 6 were waited for; matrix products, arithmetic and copies ran while one was open for 18% of the time, Pallas kernels for 0%

commit v1 on v0

v1 whole, which is shorter than its diff:
```python
import functools

import jax
import jax.numpy as jnp
from jax import lax
from jax.experimental import pallas as pl
from jax.experimental.pallas import tpu as pltpu
from jax.sharding import PartitionSpec as P

MESH = pl.DeviceIdType.MESH
NX, NY, NC, NZ = 4, 4, 2, 8
ANY = pl.BlockSpec(memory_space=pl.ANY)
VM = pl.BlockSpec(memory_space=pltpu.VMEM)
SM = pl.BlockSpec(memory_space=pltpu.SMEM)
BF = jnp.bfloat16


def coords():
    r = lax.axis_index("row")
    return r // 8, (r // 2) % 4, r % 2, lax.axis_index("col")


def column_slice(y, z):
    return (y + z // 2) % 4


def dev(y, x, c, z):
    return ((y * NX + x) * NC + c, z)


def greet(peers):
    sem = pltpu.get_barrier_semaphore()
    for peer in peers:
        pl.semaphore_signal(sem, inc=1, device_id=peer, device_id_type=MESH)
    pl.semaphore_wait(sem, len(peers))


class Links:
    def __init__(self, ss, rs):
        self.ss, self.rs, self.at, self.out = ss, rs, 0, []

    def slot(self, count=1):
        first = self.at
        self.at += count
        return first

    def send(self, i, src, dst, to):
        cp = pltpu.make_async_remote_copy(
            src_ref=src, dst_ref=dst, send_sem=self.ss.at[i], recv_sem=self.rs.at[i],
            device_id=to, device_id_type=MESH)
        cp.start()
        self.out.append(cp)

    def recv(self, i, dst, frm):
        pltpu.make_async_remote_copy(
            src_ref=dst, dst_ref=dst, send_sem=self.ss.at[i], recv_sem=self.rs.at[i],
            device_id=frm, device_id_type=MESH).wait_recv()

    def drain(self):
        for cp in self.out:
            cp.wait_send()


def ring(links, n, me, nxt, prv, view, own=None):
    steps = n // 2
    base = links.slot(4 * steps)
    own = own or (lambda h: view(me, h))
    idx = lambda d, s, h: base + (d * steps + s) * 2 + h
    for s in range(steps):
        for pos in range(1 if s == steps - 1 else 2):
            for d, h in ((0, pos), (1, 1 - pos)):
                shard = lax.rem(me + (n - s if d == 0 else s), n)
                if s:
                    yield
                    links.recv(idx(d, s - 1, h), view(shard, h), prv if d == 0 else nxt)
                src = own(h) if s == 0 else view(shard, h)
                links.send(idx(d, s, h), src, view(shard, h), nxt if d == 0 else prv)
    yield
    for s, pos in ((steps - 2, 1), (steps - 1, 0)):
        for d, h in ((0, pos), (1, 1 - pos)):
            shard = lax.rem(me + (n - s - 1 if d == 0 else s + 1), n)
            links.recv(idx(d, s, h), view(shard, h), prv if d == 0 else nxt)


def run(*gens):
    live = list(gens)
    while live:
        for g in list(live):
            try:
                next(g)
            except StopIteration:
                live.remove(g)


def remote_call(body, name, cid, outs, ins, in_specs, out_specs, nsem, scratch=(), vmem=60 * 2**20):
    return pl.pallas_call(
        body, out_shape=outs, in_specs=in_specs, out_specs=out_specs,
        scratch_shapes=[pltpu.SemaphoreType.DMA((nsem,)), pltpu.SemaphoreType.DMA((nsem,)),
                        pltpu.SemaphoreType.DMA((4,)), *scratch],
        compiler_params=pltpu.CompilerParams(
            collective_id=cid, has_side_effects=True, vmem_limit_bytes=vmem),
        name=name)(*ins)


def k1_body(low, diag, dsh, ssel, strip, dcols, dshard, s1, ss, rs, ls):
    y, x, c, z = coords()
    g = x * 2 + c
    links = Links(ss, rs)
    znext, zprev = dev(y, x, c, (z + 1) % NZ), dev(y, x, c, (z + 7) % NZ)
    line = [((g + d) % 8) for d in range(1, 8)]
    ydev = [dev((y + d) % NY, x, c, z) for d in range(1, 4)]
    ysrc = [(y + 4 - d) % NY for d in range(1, 4)]
    greet([znext, zprev] + [dev(y, q // 2, q % 2, z) for q in line] + ydev)

    def lview(shard, h):
        return strip.at[pl.ds(h * 128, 128), pl.ds(pl.multiple_of(shard * 512, 512), 512)]

    dslot = lambda t: dshard.at[pl.ds(pl.multiple_of(t * 128, 128), 128)]
    local = [
        pltpu.make_async_copy(low, strip.at[:, pl.ds(pl.multiple_of(z * 512, 512), 512)], ls.at[0]),
        pltpu.make_async_copy(diag, dcols.at[y, x, c], ls.at[1]),
        pltpu.make_async_copy(ssel.at[g], s1.at[g], ls.at[2]),
        pltpu.make_async_copy(dsh.at[column_slice(y, z)], dslot(y), ls.at[3]),
    ]
    lgen = ring(links, NZ, z, znext, zprev, lview, lambda h: low.at[pl.ds(h * 128, 128)])

    def dgen():
        sib = dev(y, x, 1 - c, z)
        xdev = [dev(y, (x + d) % NX, c, z) for d in range(1, 4)]
        xsrc = [(x + 4 - d) % NX for d in range(1, 4)]
        a, b = pl.ds(0, 64), pl.ds(64, 64)
        base = links.slot(12)
        sibs = links.slot(8)
        for d in range(3):
            links.send(base + d, diag.at[a], dcols.at[y, x, c, a], xdev[d])
            links.send(base + 3 + d, diag.at[b], dcols.at[y, x, c, b], ydev[d])
        for cp in local:
            cp.start()
        first = links.slot(14)
        for d in range(7):
            q = line[d]
            links.send(first + d, ssel.at[q], s1.at[g], dev(y, q // 2, q % 2, z))
        for d in range(3):
            t = (y + d + 1) % NY
            links.send(first + 7 + d, dsh.at[column_slice(t, z)], dslot(y), ydev[d])
        yield
        local[1].wait()
        for d in range(3):
            links.recv(base + d, dcols.at[y, xsrc[d], c, a], xdev[d])
        for d in range(3):
            links.send(base + 6 + d, dcols.at[y, :, c, a], dcols.at[y, :, c, a], ydev[d])
        links.send(sibs, dcols.at[y, :, c, a], dcols.at[y, :, c, a], sib)
        for d in range(3):
            links.recv(base + 3 + d, dcols.at[ysrc[d], x, c, b], ydev[d])
        for d in range(3):
            links.send(base + 9 + d, dcols.at[:, x, c, b], dcols.at[:, x, c, b], xdev[d])
        links.send(sibs + 1, dcols.at[:, x, c, b], dcols.at[:, x, c, b], sib)
        yield
        yield
        yield
        for d in (0, 2, 1):
            piece = dcols.at[ysrc[d], :, c, a]
            links.recv(base + 6 + d, piece, ydev[d])
            links.send(sibs + 2 + d, piece, piece, sib)
            piece = dcols.at[:, xsrc[d], c, b]
            links.recv(base + 9 + d, piece, xdev[d])
            links.send(sibs + 5 + d, piece, piece, sib)
            yield
        for d in range(7):
            s = (g + 8 - d - 1) % 8
            links.recv(first + d, s1.at[s], dev(y, s // 2, s % 2, z))
        for d in range(3):
            links.recv(first + 7 + d, dslot(ysrc[d]), ydev[d])
        yield
        o = 1 - c
        links.recv(sibs, dcols.at[y, :, o, a], sib)
        links.recv(sibs + 1, dcols.at[:, x, o, b], sib)
        for d in range(3):
            links.recv(sibs + 2 + d, dcols.at[ysrc[d], :, o, a], sib)
            links.recv(sibs + 5 + d, dcols.at[:, xsrc[d], o, b], sib)

    run(lgen, dgen())
    for k in (0, 2, 3):
        local[k].wait()
    links.drain()


def k2_body(ush, sblk, ubuf, sfull, ss, rs, ls):
    y, x, c, z = coords()
    links = Links(ss, rs)
    znext, zprev = dev(y, x, c, (z + 1) % NZ), dev(y, x, c, (z + 7) % NZ)
    ydev = [dev((y + d) % NY, x, c, z) for d in range(1, 4)]
    ysrc = [(y + 4 - d) % NY for d in range(1, 4)]
    greet([znext, zprev] + ydev)
    rows = lambda t: pl.ds(pl.multiple_of(t * 256, 256), 256)
    own = pltpu.make_async_copy(ush.at[column_slice(y, z)], ubuf.at[z, rows(y)], ls.at[0])
    base = links.slot(3)
    for d in range(3):
        links.send(base + d, ush.at[column_slice(y + d + 1, z)], ubuf.at[z, rows(y)], ydev[d])
    own.start()
    keep = pltpu.make_async_copy(sblk, sfull.at[y], ls.at[1])
    sgen = ring(links, NY, y, ydev[0], ydev[2], lambda t, h: sfull.at[t, pl.ds(h * 160, 160)],
                lambda h: sblk.at[pl.ds(h * 160, 160)])
    next(sgen)
    keep.start()
    own.wait()
    for d in range(3):
        links.recv(base + d, ubuf.at[z, rows(ysrc[d])], ydev[d])
    ugen = ring(links, NZ, z, znext, zprev, lambda t, h: ubuf.at[t, pl.ds(h * 512, 512)])
    next(ugen)
    for _ in range(4):
        next(ugen)
    run(ugen, sgen)
    keep.wait()
    links.drain()


def k3_body(part, structure, dshard, rows, dbuf, ss, rs, ls, pbuf, abuf, xbuf, fin, zbuf, snd):
    y, x, c, z = coords()
    g = x * 2 + c
    links = Links(ss, rs)
    zdev = [dev(y, x, c, (z + d) % NZ) for d in range(8)]
    sib = dev(y, x, 1 - c, z)
    plane = [(t, q) for t in range(4) for q in range(8)][1:]
    peer = lambda t, q: (((y + t) % NY) * 8 + (g + q) % 8, z)
    greet(zdev[1:] + [peer(t, q) for t, q in plane])
    order = [1, 3, 2, 0]
    base = links.slot(4)
    for d in order:
        t = (x + d) % NX
        links.send(base + d, part.at[2 * t + 1 - c], pbuf.at[d], sib)
    dgen = ring(links, NZ, z, zdev[1], zdev[7], lambda t, h: dbuf.at[t, pl.ds(h * 256, 256)],
                lambda h: dshard.at[pl.ds(h * 256, 256)])
    keep = pltpu.make_async_copy(dshard, dbuf.at[z], ls.at[0])
    keep.start()
    next(dgen)
    xs = links.slot(4)
    for d in order:
        t = (x + d) % NX
        links.recv(base + d, pbuf.at[d], sib)

        @pl.loop(0, 10)
        def _(i):
            at = pl.ds(pl.multiple_of(i * 16, 16), 16)
            total = part[2 * t + c, at].astype(jnp.float32) + pbuf[d, at].astype(jnp.float32)
            abuf[d, at] = total.astype(BF)

        if d:
            links.send(xs + d, abuf.at[d], xbuf.at[d - 1], dev(y, t, c, z))
    for _ in range(8):
        next(dgen)
    for d in (1, 3, 2):
        links.recv(xs + d, xbuf.at[d - 1], dev(y, (x + 4 - d) % NX, c, z))

    @pl.loop(0, 10)
    def _(i):
        at = pl.ds(pl.multiple_of(i * 16, 16), 16)
        total = abuf[0, at].astype(jnp.float32)
        for d in range(3):
            total = total + xbuf[d, at].astype(jnp.float32)
        total = (-total).astype(BF)
        for t in range(8):
            fin[t, i // 2, pl.ds(pl.multiple_of((i % 2) * 16, 16), 16)] = total[:, t * 128:(t + 1) * 128]

    zs = links.slot(8)
    slab = lambda k: zbuf.at[pl.ds(k * 5, 5)]
    for d in (4, 3, 5, 2, 6, 1, 7):
        links.send(zs + d, fin.at[(z + d) % NZ], slab(z), zdev[d])
    mine = pltpu.make_async_copy(fin.at[z], slab(z), ls.at[1])
    mine.start()
    for _ in dgen:
        pass
    keep.wait()
    mine.wait()
    for d in (1, 7, 2, 6, 3, 5, 4):
        links.recv(zs + d, slab((z + 8 - d) % NZ), zdev[8 - d])
    ps = links.slot(32)
    for q in range(8):
        for t in range(4):
            snd[q, t] = zbuf[structure[8 * t + q]]
    spot = lambda yy, gg: rows.at[:, gg, :, pl.ds(pl.multiple_of(column_slice(yy, z) * 128, 128), 128)]
    for t, q in plane:
        links.send(ps + 8 * t + q, snd.at[(g + q) % 8], spot(y, g), peer(t, q))
    home = pltpu.make_async_copy(snd.at[g], spot(y, g), ls.at[2])
    home.start()
    home.wait()
    for t, q in plane:
        links.recv(ps + 8 * t + q, spot((y + 4 - t) % 4, (g + 8 - q) % 8), peer(4 - t, 8 - q))
    links.drain()


def k4_body(fp, got, ss, rs, ls):
    y, x, c, z = coords()
    r = y * 8 + x * 2 + c
    g = x * 2 + c
    from_y = (r % 4 + 4 - r // 8) % 4
    is_self = from_y == y
    sem = pltpu.get_barrier_semaphore()
    dest = lambda k: 4 * k + column_slice(y, k)
    srcs = lambda q: from_y * 8 + q
    for k in range(8):
        @pl.when(dest(k) != r)
        def _():
            pl.semaphore_signal(sem, inc=1, device_id=(dest(k), z), device_id_type=MESH)

        @pl.when(srcs(k) != r)
        def _():
            pl.semaphore_signal(sem, inc=1, device_id=(srcs(k), z), device_id_type=MESH)
    pl.semaphore_wait(sem, jnp.where(is_self, 14, 16))

    def copy(k):
        return pltpu.make_async_remote_copy(
            src_ref=fp.at[k], dst_ref=got.at[g], send_sem=ss.at[k], recv_sem=rs.at[g],
            device_id=(dest(k), z), device_id_type=MESH)

    def incoming(q):
        return pltpu.make_async_remote_copy(
            src_ref=got.at[q], dst_ref=got.at[q], send_sem=ss.at[q], recv_sem=rs.at[q],
            device_id=(srcs(q), z), device_id_type=MESH)

    for k in range(8):
        @pl.when(dest(k) != r)
        def _():
            copy(k).start()

    @pl.when(is_self)
    def _():
        cp = pltpu.make_async_copy(fp.at[r // 4], got.at[g], ls.at[0])
        cp.start()
        cp.wait()

    for q in range(8):
        @pl.when(srcs(q) != r)
        def _():
            incoming(q).wait_recv()
    for k in range(8):
        @pl.when(dest(k) != r)
        def _():
            copy(k).wait_send()


def per_device(sigma_anc, lower_off, inverse_diag, structure):
    sds = jax.ShapeDtypeStruct
    blocks = sigma_anc.reshape(5, 8, 40, 256)
    ssel = jnp.take(blocks, structure, axis=2).reshape(5, 8, 4, 8, 256)
    ssel = jnp.transpose(ssel, (3, 2, 0, 1, 4)).reshape(8, 160, 256)
    dsh = jnp.transpose(inverse_diag.reshape(128, 4, 128), (1, 0, 2))
    strip, dcols, dshard, s1 = remote_call(
        k1_body, "gather_inputs", 1,
        (sds((256, 4096), BF), sds((4, 4, 2, 128, 512), BF), sds((512, 128), BF), sds((8, 160, 256), BF)),
        (lower_off, inverse_diag, dsh, ssel), [ANY] * 4, [ANY] * 4, 52)
    dmat = dcols.reshape(4096, 512)
    upper = jnp.dot(strip, dmat, preferred_element_type=jnp.float32).astype(BF)
    ush = jnp.transpose(upper.reshape(256, 4, 128), (1, 0, 2))
    sblk = jnp.transpose(s1.reshape(2, 4, 4, 5, 8, 256), (0, 3, 1, 4, 2, 5)).reshape(320, 1024)
    ubuf, sfull = remote_call(
        k2_body, "gather_upper", 2,
        (sds((8, 1024, 128), BF), sds((4, 320, 1024), BF)),
        (ush, sblk), [ANY] * 2, [ANY] * 2, 27)
    umat = jnp.transpose(ubuf, (1, 0, 2)).reshape(1024, 1024)
    part = jnp.dot(sfull.reshape(1280, 1024), umat, preferred_element_type=jnp.float32).astype(BF)
    rows, dbuf = remote_call(
        k3_body, "reduce_and_place", 3,
        (sds((4, 8, 32, 512), BF), sds((8, 512, 128), BF)),
        (part.reshape(8, 160, 1024), structure, dshard), [VM, SM, ANY], [VM, ANY], 64,
        [pltpu.VMEM((4, 160, 1024), BF), pltpu.VMEM((4, 160, 1024), BF), pltpu.VMEM((3, 160, 1024), BF),
         pltpu.VMEM((8, 5, 32, 128), BF), pltpu.VMEM((40, 32, 128), BF), pltpu.VMEM((8, 4, 32, 128), BF)])
    srows = rows.reshape(1024, 512)
    y, x, c, z = coords()
    sigma_off = lax.dynamic_slice_in_dim(srows, y * 256, 256, axis=0)
    drows = lax.dynamic_index_in_dim(dcols.reshape(4, 8, 128, 512), x * 2 + c, axis=1, keepdims=False)
    left = jnp.concatenate([ubuf, dbuf], axis=1)
    right = jnp.concatenate([-srows, drows.reshape(512, 512)], axis=0)
    fp = lax.dot_general(left, right, (((1,), (0,)), ((), ())), preferred_element_type=jnp.float32).astype(BF)
    got = remote_call(k4_body, "reduce_front", 4, sds((8, 128, 512), BF), (fp,), [ANY], ANY, 8)
    return sigma_off, jnp.sum(got.astype(jnp.float32), axis=0)


def solution(mesh):
    in_specs = (P("col", "row", None), P("row", "col"), P("row", "col"), P())
    out_specs = (P("row", "col"), P("row", "col"))
    return jax.shard_map(
        per_device, mesh=mesh, in_specs=in_specs, out_specs=out_specs, check_vma=False
    )
```

time: 447 us -> 193 us (0.43)
  waiting for transfers between devices: 304 us -> 0 us
  Pallas kernels: 0 us -> 162 us
  local copies, waits for them, and re-layouts: 60.5 us -> 12.4 us
  starting transfers between devices: 23.5 us -> 0 us
  blocking collectives: 17.3 us -> 0 us
  between operations: 14.3 us -> 0.81 us
  matrix products: 18.8 us -> 13 us
    all_gather x6 -> x0, waiting for transfers between devices: 169 us -> none  [the longest x1 54.7 us: per_device(): upper_all = lax.all_gather(upper, 'row', axis=0, tiled=True)]
    pallas_call x0 -> x4, Pallas kernels: none -> 162 us  [remote_call(): pl.pallas_call(body, out_shape=outs, in_specs=in_specs, out_specs=out_spe...]
    all_to_all x3 -> x0, waiting for transfers between devices: 133 us -> none  [the longest x1 108 us: per_device(): lax.all_to_all(outgoing, 'col', split_axis=0, concat_axis=0, tiled=True)]
    all_to_all x3 -> x0, starting transfers between devices: 23.3 us -> none  [the longest x1 8.47 us: per_device(): lax.all_to_all(outgoing, 'col', split_axis=0, concat_axis=0, tiled=True)]
    unnamed x15 -> x9, local copies, waits for them, and re-layouts: 23.3 us -> 2.12 us
    all_to_all x1 -> x0, blocking collectives: 17.3 us -> none  [per_device(): lax.all_to_all(own_rows, 'row', split_axis=2, concat_axis=1, tiled=True)]
    all_to_all x3 -> x0, local copies, waits for them, and re-layouts: 16.8 us -> none  [the longest x1 11 us: per_device(): lax.all_to_all(own_rows, 'row', split_axis=2, concat_axis=1, tiled=True)]
    gather x5 -> x1, local copies, waits for them, and re-layouts: 14.7 us -> 0.63 us  [per_device(): ssel = jnp.take(blocks, structure, axis=2).reshape(5, 8, 4, 8, 256)]
  transfers between devices with their start and end apart: 9 -> 0, of which waited for: 6 -> 0; matrix products, arithmetic and copies ran while one was open for 18% -> 0% of each run, Pallas kernels for 0% -> 0%
where the time goes in v1:
time: 193 us
  Pallas kernels  162 us (84%)
  matrix products  13 us (7%)
  local copies, waits for them, and re-layouts  12.4 us (6%)
  other arithmetic  4.87 us (3%)
    pallas_call x4, Pallas kernels, remote_call(): pl.pallas_call(body, out_shape=outs, in_specs=in_specs, out_specs=out_spe...  162 us
    dot_general x1, matrix products, per_device(): jnp.dot(sfull.reshape(1280, 1024), umat, preferred_element_type=jnp.float32)  6.07 us
    dot_general x1, matrix products, per_device(): upper = jnp.dot(strip, dmat, preferred_element_type=jnp.float32).astype(BF)  4.12 us

profile of v1, /device:TPU:24, one launch (start us, length us, event | category | flops | bytes accessed | tf_op | source)
XLA Modules:
  0.0 193.0 jit_solution(3686503294171063023)
XLA Ops:
  0.6 0.0 copy-start
  0.7 1.1 copy-done
  1.8 0.7 compare_and_fusion
  2.4 0.1 broadcast_in_dim.14
  2.5 0.7 compare_select_fusion
  3.2 1.0 copy.17
  4.2 0.8 copy.18
  5.0 0.6 gather_fusion
  5.6 0.2 fusion.9
  5.8 1.2 copy.20
  7.0 43.1 %gather_inputs.1 = (bf16[256,4096]{1,0:T(8,128)(2,1)}, bf16[4,4,2,128,512]{4,3,2,1,0:T(8,128)(2,1)}, bf16[512,128]{1,0:T(8,128)(2,1)}, bf16[8,160,256]{2,1,0:T(8,128)(2,1)}) custom-call(bf16[256,512]{1,0:T(8,128)(2,1)} %low.1, bf16[128,512]{1,0:T(8,128)(2,1)} %diag.1, bf16[4,128,128]{2,1,0:T(8,128)(2,1)} %bitcast.46, bf16[8,160,256]{2,1,0:T(8,128)(2,1)} %bitcast.38), custom_call_target="tpu_custom_call" | custom-call | tf_op jit(solution)/shard_map/gather_inputs/pallas_call | solution.py:96
  50.1 0.0 copy-start.2
  50.1 4.1 %convolution_convert_fusion.1 = bf16[256,512]{1,0:T(8,128)(2,1)S(1)} fusion(bf16[256,4096]{1,0:T(8,128)(2,1)} %get-tuple-element.10, bf16[4096,512]{1,0:T(8,128)(2,1)} %bitcast.49), kind=kOutput, calls=%fused_computation.11 | convolution fusion | flops 1073872896 | bytes 6553600 | tf_op jit(solution)/shard_map/dot_general | solution.py:353
  54.2 0.1 copy.21
  54.4 0.8 copy.22
  55.2 0.0 copy-done.2
  55.2 0.9 copy.23
  56.1 1.1 constant_dynamic-slice_fusion
  57.2 35.2 %gather_upper.1 = (bf16[8,1024,128]{2,1,0:T(8,128)(2,1)}, bf16[4,320,1024]{2,1,0:T(8,128)(2,1)}) custom-call(bf16[4,256,128]{2,1,0:T(8,128)(2,1)} %bitcast.43, bf16[320,1024]{1,0:T(8,128)(2,1)} %bitcast.37), custom_call_target="tpu_custom_call" | custom-call | tf_op jit(solution)/shard_map/gather_upper/pallas_call | solution.py:96
  92.4 2.9 %copy.24 = bf16[1024,8,128]{0,2,1:T(8,128)(2,1)S(1)} copy(bf16[1024,8,128]{2,0,1:T(8,128)(2,1)} %bitcast.40) | data formatting | bytes 4194304 | tf_op jit(solution)/shard_map/transpose | solution.py:360
  95.3 6.1 %convolution_convert_fusion = bf16[1280,1024]{1,0:T(8,128)(2,1)} fusion(bf16[1280,1024]{1,0:T(8,128)(2,1)} %bitcast.51, bf16[1024,1024]{0,1:T(8,128)(2,1)S(1)} %bitcast.41), kind=kOutput, calls=%fused_computation.1 | convolution fusion | flops 2685665280 | bytes 7340032 | tf_op jit(solution)/shard_map/dot_general | solution.py:361
  101.4 0.0 copy-start.1
  101.4 55.5 %reduce_and_place.1 = (bf16[4,8,32,512]{3,2,1,0:T(8,128)(2,1)}, bf16[8,512,128]{2,1,0:T(8,128)(2,1)}) custom-call(bf16[8,160,1024]{2,1,0:T(8,128)(2,1)} %bitcast.36, s32[32]{0:T(128)} %structure.1, bf16[512,128]{1,0:T(8,128)(2,1)} %get-tuple-element.15.dshard), custom_call_target="tpu_custom_call" | custom-call | tf_op jit(solution)/shard_map/reduce_and_place/pallas_call | solution.py:96
  156.9 0.0 copy-start.3
  156.9 1.8 constant_dynamic-slice_fusion.1
  158.6 1.3 bitcast_negate_fusion
  159.9 0.0 copy-done.1
  159.9 0.0 copy-done.3
  160.0 2.8 %fusion.6.fp = bf16[8,128,512]{2,1,0:T(8,128)(2,1)} fusion(bf16[512,512]{1,0:T(8,128)(2,1)S(1)} %bitcast.48, bf16[1024,512]{1,0:T(8,128)(2,1)S(1)} %bitcast_negate_fusion, bf16[8,512,128]{2,1,0:T(8,128)(2,1)S(1)} %copy-done.3, bf16[8,1024,128]{2,1,0:T(8,128)(2,1)S(1)} %copy-done.1), kind=kOutput, calls=%fused_computation.10 | convolution fusion | flops 1620574208 | bytes 5767168 | tf_op jit(solution)/shard_map/dot_general | solution.py:374
  162.8 28.1 %reduce_front.1 = bf16[8,128,512]{2,1,0:T(8,128)(2,1)} custom-call(bf16[8,128,512]{2,1,0:T(8,128)(2,1)} %fusion.6.fp), custom_call_target="tpu_custom_call" | custom-call | tf_op jit(solution)/shard_map/reduce_front/pallas_call | solution.py:96
  190.9 2.1 %convert_reduce_fusion = f32[128,512]{1,0:T(8,128)} fusion(bf16[8,128,512]{2,1,0:T(8,128)(2,1)} %reduce_front.1), kind=kLoop, calls=%fused_computation.6 | loop fusion | flops 983040 | bytes 1310720 | tf_op jit(solution)/shard_map/reduce_sum | solution.py:376
  (1 shorter events, 0.0 us)
Async XLA Ops:
  0.6 1.2 copy-start
  50.1 5.1 %copy-start.2 = (bf16[8,160,256]{2,1,0:T(8,128)(2,1)S(1)}, bf16[8,160,256]{2,1,0:T(8,128)(2,1)}, u32[]{:S(2)}) copy-start(bf16[8,160,256]{2,1,0:T(8,128)(2,1)} %get-tuple-element.12) | copy-start | bytes 1966084
  101.4 58.6 %copy-start.1 = (bf16[8,1024,128]{2,1,0:T(8,128)(2,1)S(1)}, bf16[8,1024,128]{2,1,0:T(8,128)(2,1)}, u32[]{:S(2)}) copy-start(bf16[8,1024,128]{2,1,0:T(8,128)(2,1)} %get-tuple-element.14) | copy-start | bytes 6291460
  156.9 3.1 %copy-start.3 = (bf16[8,512,128]{2,1,0:T(8,128)(2,1)S(1)}, bf16[8,512,128]{2,1,0:T(8,128)(2,1)}, u32[]{:S(2)}) copy-start(bf16[8,512,128]{2,1,0:T(8,128)(2,1)} %get-tuple-element.17) | copy-start | bytes 3145732

commit v2 on v0

v2 whole, which is shorter than its diff:
```python
import functools

import jax
import jax.numpy as jnp
from jax import lax
from jax.experimental import pallas as pl
from jax.experimental.pallas import tpu as pltpu
from jax.sharding import PartitionSpec as P

MESH = pl.DeviceIdType.MESH
NX, NY, NC, NZ = 4, 4, 2, 8
ANY = pl.BlockSpec(memory_space=pl.ANY)
VM = pl.BlockSpec(memory_space=pltpu.VMEM)
SM = pl.BlockSpec(memory_space=pltpu.SMEM)
BF = jnp.bfloat16


def coords():
    r = lax.axis_index("row")
    return r // 8, (r // 2) % 4, r % 2, lax.axis_index("col")


def column_slice(y, z):
    return (y + z // 2) % 4


def dev(y, x, c, z):
    return ((y * NX + x) * NC + c, z)


def greet(peers):
    sem = pltpu.get_barrier_semaphore()
    for peer in peers:
        pl.semaphore_signal(sem, inc=1, device_id=peer, device_id_type=MESH)
    pl.semaphore_wait(sem, len(peers))


class Links:
    def __init__(self, ss, rs):
        self.ss, self.rs, self.at, self.out = ss, rs, 0, []

    def slot(self, count=1):
        first = self.at
        self.at += count
        return first

    def send(self, i, src, dst, to):
        cp = pltpu.make_async_remote_copy(
            src_ref=src, dst_ref=dst, send_sem=self.ss.at[i], recv_sem=self.rs.at[i],
            device_id=to, device_id_type=MESH)
        cp.start()
        self.out.append(cp)

    def recv(self, i, dst, frm):
        pltpu.make_async_remote_copy(
            src_ref=dst, dst_ref=dst, send_sem=self.ss.at[i], recv_sem=self.rs.at[i],
            device_id=frm, device_id_type=MESH).wait_recv()

    def drain(self):
        for cp in self.out:
            cp.wait_send()


def ring(links, n, me, nxt, prv, view, own=None):
    steps = n // 2
    base = links.slot(4 * steps)
    own = own or (lambda h: view(me, h))
    idx = lambda d, s, h: base + (d * steps + s) * 2 + h
    for s in range(steps):
        for pos in range(1 if s == steps - 1 else 2):
            for d, h in ((0, pos), (1, 1 - pos)):
                shard = lax.rem(me + (n - s if d == 0 else s), n)
                if s:
                    yield
                    links.recv(idx(d, s - 1, h), view(shard, h), prv if d == 0 else nxt)
                src = own(h) if s == 0 else view(shard, h)
                links.send(idx(d, s, h), src, view(shard, h), nxt if d == 0 else prv)
    yield
    for s, pos in ((steps - 2, 1), (steps - 1, 0)):
        for d, h in ((0, pos), (1, 1 - pos)):
            shard = lax.rem(me + (n - s - 1 if d == 0 else s + 1), n)
            links.recv(idx(d, s, h), view(shard, h), prv if d == 0 else nxt)
        if pos:
            yield


def pull(gen):
    try:
        next(gen)
        return True
    except StopIteration:
        return False


def run(*gens):
    live = list(gens)
    while live:
        for g in list(live):
            try:
                next(g)
            except StopIteration:
                live.remove(g)


def mega(low, diag, dsh, ssel, structure, sig, front, ss, rs, ls,
         strip, dcols, dshard, s1, sblk, sfull, acc, ush, ubuf, dbuf,
         part, pbuf, abuf, xbuf, fin, zbuf, snd, rows, fp, got):
    y, x, c, z = coords()
    g = x * 2 + c
    r = y * 8 + g
    links = Links(ss, rs)
    zdev = [dev(y, x, c, (z + d) % NZ) for d in range(8)]
    xdev = [dev(y, (x + d) % NX, c, z) for d in range(4)]
    ydev = [dev((y + d) % NY, x, c, z) for d in range(4)]
    ysrc = [(y + 4 - d) % NY for d in range(4)]
    sib = dev(y, x, 1 - c, z)
    plane = [(t, q) for t in range(4) for q in range(8)][1:]
    peer = lambda t, q: (((y + t) % NY) * 8 + (g + q) % 8, z)
    greet(zdev[1:] + [peer(t, q) for t, q in plane])

    a, b = pl.ds(0, 64), pl.ds(64, 64)
    dslot = lambda t: dshard.at[pl.ds(pl.multiple_of(t * 128, 128), 128)]
    local = [
        pltpu.make_async_copy(low, strip.at[z], ls.at[0]),
        pltpu.make_async_copy(diag, dcols.at[y, x, c], ls.at[1]),
        pltpu.make_async_copy(ssel.at[g], s1.at[g], ls.at[2]),
        pltpu.make_async_copy(dsh.at[column_slice(y, z)], dslot(y), ls.at[3]),
    ]
    lgen = ring(links, NZ, z, zdev[1], zdev[7], lambda t, h: strip.at[t, pl.ds(h * 128, 128)],
                lambda h: low.at[pl.ds(h * 128, 128)])
    pull(lgen)
    a1 = ring(links, NY, y, ydev[1], ydev[3], lambda t, h: dcols.at[t, x, c, pl.ds(h * 32, 32)],
              lambda h: diag.at[pl.ds(h * 32, 32)])
    b1 = ring(links, NX, x, xdev[1], xdev[3], lambda t, h: dcols.at[y, t, c, pl.ds(64 + h * 32, 32)],
              lambda h: diag.at[pl.ds(64 + h * 32, 32)])
    pull(a1)
    pull(b1)
    for cp in (local[1], local[0], local[2], local[3]):
        cp.start()
    run(a1, b1)
    local[1].wait()
    a2 = ring(links, NX, x, xdev[1], xdev[3], lambda t, h: dcols.at[pl.ds(2 * h, 2), t, c, a])
    b2 = ring(links, NY, y, ydev[1], ydev[3], lambda t, h: dcols.at[t, pl.ds(2 * h, 2), c, b])
    pull(a2)
    pull(b2)
    first = links.slot(10)
    for d in (3, 2, 4, 1, 5, 0, 6):
        q = (g + d + 1) % 8
        links.send(first + d, ssel.at[q], s1.at[g], dev(y, q // 2, q % 2, z))
    for d in range(3):
        links.send(first + 7 + d, dsh.at[column_slice(y + d + 1, z)], dslot(y), ydev[d + 1])
    sibs = links.slot(8)

    def share(k, d):
        t = (x + 4 - d) % NX
        links.send(sibs + k, dcols.at[:, t, c, a], dcols.at[:, t, c, a], sib)
        t = ysrc[d]
        links.send(sibs + k + 1, dcols.at[t, :, c, b], dcols.at[t, :, c, b], sib)

    share(0, 0)
    for _ in range(2):
        pull(lgen)
        pull(lgen)
        pull(a2)
        pull(b2)
    for _ in range(2):
        pull(lgen)
        pull(lgen)
    pull(a2)
    pull(b2)
    share(2, 1)
    share(4, 3)
    for _ in range(2):
        pull(lgen)
    pull(a2)
    pull(b2)
    share(6, 2)

    local[2].wait()
    for d in range(7):
        s = (g + 8 - d - 1) % 8
        links.recv(first + d, s1.at[s], dev(y, s // 2, s % 2, z))

    @pl.loop(0, 2)
    def _(h):
        parts = [s1[4 * h + q].astype(jnp.float32).reshape(4, 5, 8, 256) for q in range(4)]
        for kb in range(4):
            for blk in range(5):
                tile = jnp.concatenate([p[kb, blk] for p in parts], axis=0).astype(BF)
                at = pl.ds(pl.multiple_of(h * 160 + blk * 32, 32), 32)
                sblk[at, kb * 256:(kb + 1) * 256] = tile

    keep = pltpu.make_async_copy(sblk, sfull.at[y], ls.at[2])
    keep.start()
    sgen = ring(links, NY, y, ydev[1], ydev[3], lambda t, h: sfull.at[t, pl.ds(h * 160, 160)],
                lambda h: sblk.at[pl.ds(h * 160, 160)])
    pull(sgen)
    while pull(lgen):
        pass
    for k, d in ((0, 0), (2, 1), (4, 3), (6, 2)):
        t = (x + 4 - d) % NX
        links.recv(sibs + k, dcols.at[:, t, 1 - c, a], sib)
        t = ysrc[d]
        links.recv(sibs + k + 1, dcols.at[t, :, 1 - c, b], sib)
    local[0].wait()

    acc[...] = jnp.zeros_like(acc)

    @pl.loop(0, 8)
    def _(k):
        right = dcols[k // 2, pl.ds((k % 2) * 2, 2)].reshape(512, 512)
        acc[...] += jnp.dot(strip[k], right, preferred_element_type=jnp.float32)

    for j in range(4):
        ush[j] = acc[:, j * 128:(j + 1) * 128].astype(BF)

    kblock = lambda t: pl.ds(pl.multiple_of(t * 256, 256), 256)
    own = pltpu.make_async_copy(ush.at[column_slice(y, z)], ubuf.at[z, kblock(y)], ls.at[0])
    base = links.slot(3)
    for d in range(3):
        links.send(base + d, ush.at[column_slice(y + d + 1, z)], ubuf.at[z, kblock(y)], ydev[d + 1])
    own.start()
    own.wait()
    for d in range(3):
        links.recv(base + d, ubuf.at[z, kblock(ysrc[d + 1])], ydev[3 - d])
    ugen = ring(links, NZ, z, zdev[1], zdev[7], lambda t, h: ubuf.at[t, pl.ds(h * 512, 512)])
    pull(ugen)
    local[3].wait()
    for d in range(3):
        links.recv(first + 7 + d, dslot(ysrc[d + 1]), ydev[3 - d])

    pair, xs, zs = links.slot(5), links.slot(15), links.slot(8)
    slab = lambda k: zbuf.at[pl.ds(k * 5, 5)]
    zkeep = pltpu.make_async_copy(fin.at[z], slab(z), ls.at[1])

    def shards(k):
        return ((z,), *[((z + d) % NZ, (z + NZ - d) % NZ) for d in (1, 2, 3)], ((z + 4) % NZ,))[k]

    def multiply(k):
        ids = shards(k)
        n = 128 * len(ids)
        right = jnp.concatenate([ubuf[t] for t in ids], axis=1) if len(ids) == 2 else ubuf[ids[0]]

        @pl.loop(0, 4)
        def _(i):
            total = jnp.dot(sfull[i], right, preferred_element_type=jnp.float32).astype(BF)
            part[k, i, 0, :, :n] = total[:160]
            part[k, i, 1, :, :n] = total[160:]

        links.send(pair + k, part.at[k, :, 1 - c, :, pl.ds(0, n)], pbuf.at[k, :, :, pl.ds(0, n)], sib)

    def across(k):
        n = 128 * len(shards(k))
        links.recv(pair + k, pbuf.at[k, :, :, pl.ds(0, n)], sib)

        @pl.loop(0, 4)
        def _(i):
            @pl.loop(0, 5)
            def _(j):
                at = pl.ds(pl.multiple_of(j * 32, 32), 32)
                total = part[k, i, c, at, :n].astype(jnp.float32) + pbuf[k, i, at, :n].astype(jnp.float32)
                abuf[k, i, at, :n] = total.astype(BF)

        for d in (2, 1, 3):
            links.send(xs + 3 * k + d - 1, abuf.at[k, (x + d) % NX, :, pl.ds(0, n)],
                       xbuf.at[k, d - 1, :, pl.ds(0, n)], xdev[d])

    def onward(k):
        ids = shards(k)
        n = 128 * len(ids)
        for d in (1, 3, 2):
            links.recv(xs + 3 * k + d - 1, xbuf.at[k, d - 1, :, pl.ds(0, n)], xdev[4 - d])

        @pl.loop(0, 5)
        def _(j):
            at = pl.ds(pl.multiple_of(j * 32, 32), 32)
            total = abuf[k, x, at, :n].astype(jnp.float32)
            for d in range(3):
                total = total + xbuf[k, d, at, :n].astype(jnp.float32)
            total = (-total).astype(BF)
            for m, t in enumerate(ids):
                fin[t, j] = total[:, m * 128:(m + 1) * 128]

        if k == 0:
            zkeep.start()
        else:
            for d in sorted({k, NZ - k}):
                links.send(zs + d, fin.at[(z + d) % NZ], slab(z), zdev[d])

    pull(sgen)
    pull(sgen)
    for _ in range(4):
        pull(ugen)
    while pull(sgen):
        pass
    keep.wait()
    multiply(0)
    multiply(1)
    across(0)
    for _ in range(4):
        pull(ugen)
    multiply(2)
    across(1)
    onward(0)
    for _ in range(3):
        pull(ugen)
    multiply(3)
    across(2)
    onward(1)
    pull(ugen)
    multiply(4)
    across(3)
    onward(2)
    across(4)
    onward(3)
    onward(4)
    dgen = ring(links, NZ, z, zdev[1], zdev[7], lambda t, h: dbuf.at[t, pl.ds(h * 256, 256)],
                lambda h: dshard.at[pl.ds(h * 256, 256)])
    dkeep = pltpu.make_async_copy(dshard, dbuf.at[z], ls.at[0])
    dkeep.start()
    pull(dgen)
    for _ in range(4):
        pull(dgen)
    zkeep.wait()
    for d in (1, 7, 2, 6, 3, 5, 4):
        links.recv(zs + d, slab((z + 8 - d) % NZ), zdev[8 - d])

    ps = links.slot(32)
    for q in range(8):
        for t in range(4):
            snd[q, t] = zbuf[structure[8 * t + q]]
    spot = lambda yy, gg: rows.at[:, gg, :, pl.ds(pl.multiple_of(column_slice(yy, z) * 128, 128), 128)]
    for t, q in plane:
        links.send(ps + 8 * t + q, snd.at[(g + q) % 8], spot(y, g), peer(t, q))
    home = pltpu.make_async_copy(snd.at[g], spot(y, g), ls.at[3])
    home.start()
    while pull(dgen):
        pass
    home.wait()
    dkeep.wait()
    for t, q in plane:
        links.recv(ps + 8 * t + q, spot((y + 4 - t) % 4, (g + 8 - q) % 8), peer(4 - t, 8 - q))
    sig[...] = rows[y].reshape(256, 512)

    fs = links.slot(8)
    from_y = (r % 4 + 4 - y) % 4
    is_self = from_y == y
    dest = lambda k: 4 * k + column_slice(y, k)
    src = lambda q: from_y * 8 + q

    def outgoing(k):
        return pltpu.make_async_remote_copy(
            src_ref=fp.at[k], dst_ref=got.at[g], send_sem=ss.at[fs + k], recv_sem=rs.at[fs + g],
            device_id=(dest(k), z), device_id_type=MESH)

    def incoming(q):
        return pltpu.make_async_remote_copy(
            src_ref=got.at[q], dst_ref=got.at[q], send_sem=ss.at[fs + q], recv_sem=rs.at[fs + q],
            device_id=(src(q), z), device_id_type=MESH)

    drows = dcols[:, x, c].reshape(512, 512)
    srows = rows[...].reshape(1024, 512)
    over_rows = (((0,), (0,)), ((), ()))
    for k in range(8):
        fp[k] = (
            lax.dot_general(dbuf[k], drows, over_rows, preferred_element_type=jnp.float32)
            - lax.dot_general(ubuf[k], srows, over_rows, preferred_element_type=jnp.float32)
        ).astype(BF)

        @pl.when(dest(k) != r)
        def _():
            outgoing(k).start()

    @pl.when(is_self)
    def _():
        got[g] = fp[r // 4]

    front[...] = jnp.zeros_like(front)
    for q in range(8):
        @pl.when(src(q) != r)
        def _():
            incoming(q).wait_recv()

        front[...] += got[q].astype(jnp.float32)
    for k in range(8):
        @pl.when(dest(k) != r)
        def _():
            outgoing(k).wait_send()
    links.drain()


def per_device(sigma_anc, lower_off, inverse_diag, structure):
    blocks = sigma_anc.reshape(5, 8, 40, 256)
    ssel = jnp.take(blocks, structure, axis=2).reshape(5, 8, 4, 8, 256)
    ssel = jnp.transpose(ssel, (3, 2, 0, 1, 4)).reshape(8, 160, 256)
    dsh = jnp.transpose(inverse_diag.reshape(128, 4, 128), (1, 0, 2))
    nsem = 210
    return pl.pallas_call(
        mega,
        out_shape=(jax.ShapeDtypeStruct((256, 512), BF), jax.ShapeDtypeStruct((128, 512), jnp.float32)),
        in_specs=[ANY] * 4 + [SM], out_specs=[VM, VM],
        scratch_shapes=[
            pltpu.SemaphoreType.DMA((nsem,)), pltpu.SemaphoreType.DMA((nsem,)), pltpu.SemaphoreType.DMA((4,)),
            pltpu.VMEM((8, 256, 512), BF), pltpu.VMEM((4, 4, 2, 128, 512), BF), pltpu.VMEM((512, 128), BF),
            pltpu.VMEM((8, 160, 256), BF), pltpu.VMEM((320, 1024), BF), pltpu.VMEM((4, 320, 1024), BF),
            pltpu.VMEM((256, 512), jnp.float32), pltpu.VMEM((4, 256, 128), BF), pltpu.VMEM((8, 1024, 128), BF),
            pltpu.VMEM((8, 512, 128), BF),
            pltpu.VMEM((5, 4, 2, 160, 256), BF), pltpu.VMEM((5, 4, 160, 256), BF),
            pltpu.VMEM((5, 4, 160, 256), BF), pltpu.VMEM((5, 3, 160, 256), BF),
            pltpu.VMEM((8, 5, 32, 128), BF), pltpu.VMEM((40, 32, 128), BF), pltpu.VMEM((8, 4, 32, 128), BF),
            pltpu.VMEM((4, 8, 32, 512), BF), pltpu.VMEM((8, 128, 512), BF), pltpu.VMEM((8, 128, 512), BF)],
        compiler_params=pltpu.CompilerParams(
            collective_id=1, has_side_effects=True, vmem_limit_bytes=60 * 2**20),
        name="selected_inverse")(lower_off, inverse_diag, dsh, ssel, structure)


def solution(mesh):
    in_specs = (P("col", "row", None), P("row", "col"), P("row", "col"), P())
    out_specs = (P("row", "col"), P("row", "col"))
    return jax.shard_map(
        per_device, mesh=mesh, in_specs=in_specs, out_specs=out_specs, check_vma=False
    )
```

time: 447 us -> 145 us (0.32)
  waiting for transfers between devices: 304 us -> 0 us
  Pallas kernels: 0 us -> 136 us
  local copies, waits for them, and re-layouts: 60.5 us -> 6.31 us
  starting transfers between devices: 23.5 us -> 0 us
  matrix products: 18.8 us -> 0 us
  blocking collectives: 17.3 us -> 0 us
  between operations: 14.3 us -> 0.69 us
  other arithmetic: 6.31 us -> 0.91 us
    all_gather x6 -> x0, waiting for transfers between devices: 169 us -> none  [the longest x1 54.7 us: per_device(): upper_all = lax.all_gather(upper, 'row', axis=0, tiled=True)]
    pallas_call x0 -> x1, Pallas kernels: none -> 136 us  [per_device(): pl.pallas_call(mega, out_shape=(jax.ShapeDtypeStruct((256, 512), BF), jax...]
    all_to_all x3 -> x0, waiting for transfers between devices: 133 us -> none  [the longest x1 108 us: per_device(): lax.all_to_all(outgoing, 'col', split_axis=0, concat_axis=0, tiled=True)]
    all_to_all x3 -> x0, starting transfers between devices: 23.3 us -> none  [the longest x1 8.47 us: per_device(): lax.all_to_all(outgoing, 'col', split_axis=0, concat_axis=0, tiled=True)]
    unnamed x15 -> x11, local copies, waits for them, and re-layouts: 23.3 us -> 3.61 us
    dot_general x4 -> x0, matrix products: 18.8 us -> none  [the longest x1 7.71 us: per_device(): jnp.dot(strip, upper_all, preferred_element_type=jnp.float32)]
    all_to_all x1 -> x0, blocking collectives: 17.3 us -> none  [per_device(): lax.all_to_all(own_rows, 'row', split_axis=2, concat_axis=1, tiled=True)]
    all_to_all x3 -> x0, local copies, waits for them, and re-layouts: 16.8 us -> none  [the longest x1 11 us: per_device(): lax.all_to_all(own_rows, 'row', split_axis=2, concat_axis=1, tiled=True)]
  transfers between devices with their start and end apart: 9 -> 0, of which waited for: 6 -> 0; matrix products, arithmetic and copies ran while one was open for 18% -> 0% of each run, Pallas kernels for 0% -> 0%
where the time goes in v2:
time: 145 us; the launch traced here: 144 us
  Pallas kernels  136 us (94%)
  local copies, waits for them, and re-layouts  6.31 us (4%)
    pallas_call x1, Pallas kernels, per_device(): pl.pallas_call(mega, out_shape=(jax.ShapeDtypeStruct((256, 512), BF), jax...  136 us
    unnamed x11, local copies, waits for them, and re-layouts  3.61 us

profile of v2, /device:TPU:24, one launch (start us, length us, event | category | flops | bytes accessed | tf_op | source)
XLA Modules:
  0.0 143.5 jit_solution(13000629632188930305)
XLA Ops:
  0.6 0.0 copy-start
  0.6 0.7 compare_select_fusion
  1.4 0.4 copy-done
  1.8 0.6 gather_fusion
  2.4 0.0 copy-start.3
  2.4 0.6 copy-done.3
  3.1 0.1 broadcast_in_dim.14
  3.2 0.2 fusion
  3.3 0.0 copy-start.1
  3.4 1.2 copy.13
  4.6 0.0 copy-done.1
  4.6 0.1 copy.10
  4.7 0.8 copy.11
  5.5 135.6 %selected_inverse.1 = (bf16[256,512]{1,0:T(8,128)(2,1)}, f32[128,512]{1,0:T(8,128)}) custom-call(bf16[256,512]{1,0:T(8,128)(2,1)} %low.1, bf16[128,512]{1,0:T(8,128)(2,1)} %diag.1, bf16[4,128,128]{2,1,0:T(8,128)(2,1)} %bitcast.14, bf16[8,160,256]{2,1,0:T(8,128)(2,1)} %bitcast.12, s32[32]{0:T(128)} %structure.1), custom_call_target="tpu_custom_call" | custom-call | tf_op jit(solution)/shard_map/selected_inverse/pallas_call | solution.py:398
  141.1 0.0 copy-start.2
  141.1 1.7 %copy.17 = bf16[256,512]{1,0:T(8,128)(2,1)} copy(bf16[256,512]{1,0:T(8,128)(2,1)} %get-tuple-element.4) | data formatting | bytes 524288
  142.8 0.0 copy-done.2
  142.8 0.7 copy.18
  (2 shorter events, 0.0 us)
Async XLA Ops:
  0.6 1.2 copy-start
  2.4 0.7 copy-start.3
  3.3 1.2 copy-start.1
  141.1 1.7 %copy-start.2 = (f32[128,512]{1,0:T(8,128)S(1)}, f32[128,512]{1,0:T(8,128)}, u32[]{:S(2)}) copy-start(f32[128,512]{1,0:T(8,128)} %get-tuple-element.5) | copy-start | bytes 786436

commit v3 on v2

--- a/solution.py
+++ b/solution.py
@@ -61,13 +61,15 @@
             cp.wait_send()
 
 
-def ring(links, n, me, nxt, prv, view, own=None):
+def ring(links, n, me, nxt, prv, view, own=None, pause=False):
     steps = n // 2
     base = links.slot(4 * steps)
     own = own or (lambda h: view(me, h))
     idx = lambda d, s, h: base + (d * steps + s) * 2 + h
     for s in range(steps):
         for pos in range(1 if s == steps - 1 else 2):
+            if pause and s == 0 and pos == 1:
+                yield
             for d, h in ((0, pos), (1, 1 - pos)):
                 shard = lax.rem(me + (n - s if d == 0 else s), n)
                 if s:
@@ -102,9 +104,19 @@
                 live.remove(g)
 
 
-def mega(low, diag, dsh, ssel, structure, sig, front, ss, rs, ls,
+def choose(anc, structure, ssel):
+    for q in range(8):
+        picked = []
+        for t in range(4):
+            at = pl.ds(pl.multiple_of(structure[8 * t + q] * 256, 256), 256)
+            picked.append(anc[:, :, at].astype(jnp.float32).reshape(40, 256))
+        ssel[q] = jnp.concatenate(picked, axis=0).astype(BF)
+
+
+def mega(low, diag, ssel, structure, sig, front, ss, rs, ls,
+
          strip, dcols, dshard, s1, sblk, sfull, acc, ush, ubuf, dbuf,
-         part, pbuf, abuf, xbuf, fin, zbuf, snd, rows, fp, got):
+         part, pbuf, abuf, xbuf, fin, zbuf, snd, rows, fp, got, fpd, utr):
     y, x, c, z = coords()
     g = x * 2 + c
     r = y * 8 + g
@@ -116,15 +128,16 @@
     sib = dev(y, x, 1 - c, z)
     plane = [(t, q) for t in range(4) for q in range(8)][1:]
     peer = lambda t, q: (((y + t) % NY) * 8 + (g + q) % 8, z)
-    greet(zdev[1:] + [peer(t, q) for t, q in plane])
+    greet([zdev[1], zdev[7]] + [peer(0, q) for q in range(1, 8)] + ydev[1:])
 
     a, b = pl.ds(0, 64), pl.ds(64, 64)
     dslot = lambda t: dshard.at[pl.ds(pl.multiple_of(t * 128, 128), 128)]
+    dsl = lambda t: diag.at[:, pl.ds(pl.multiple_of(column_slice(t, z) * 128, 128), 128)]
     local = [
         pltpu.make_async_copy(low, strip.at[z], ls.at[0]),
         pltpu.make_async_copy(diag, dcols.at[y, x, c], ls.at[1]),
         pltpu.make_async_copy(ssel.at[g], s1.at[g], ls.at[2]),
-        pltpu.make_async_copy(dsh.at[column_slice(y, z)], dslot(y), ls.at[3]),
+        pltpu.make_async_copy(dsl(y), dslot(y), ls.at[3]),
     ]
     lgen = ring(links, NZ, z, zdev[1], zdev[7], lambda t, h: strip.at[t, pl.ds(h * 128, 128)],
                 lambda h: low.at[pl.ds(h * 128, 128)])
@@ -135,8 +148,9 @@
               lambda h: diag.at[pl.ds(64 + h * 32, 32)])
     pull(a1)
     pull(b1)
-    for cp in (local[1], local[0], local[2], local[3]):
+    for cp in (local[1], local[0], local[3]):
         cp.start()
+    local[2].start()
     run(a1, b1)
     local[1].wait()
     a2 = ring(links, NX, x, xdev[1], xdev[3], lambda t, h: dcols.at[pl.ds(2 * h, 2), t, c, a])
@@ -148,7 +162,7 @@
         q = (g + d + 1) % 8
         links.send(first + d, ssel.at[q], s1.at[g], dev(y, q // 2, q % 2, z))
     for d in range(3):
-        links.send(first + 7 + d, dsh.at[column_slice(y + d + 1, z)], dslot(y), ydev[d + 1])
+        links.send(first + 7 + d, dsl(y + d + 1), dslot(y), ydev[d + 1])
     sibs = links.slot(8)
 
     def share(k, d):
@@ -193,8 +207,16 @@
     keep = pltpu.make_async_copy(sblk, sfull.at[y], ls.at[2])
     keep.start()
     sgen = ring(links, NY, y, ydev[1], ydev[3], lambda t, h: sfull.at[t, pl.ds(h * 160, 160)],
-                lambda h: sblk.at[pl.ds(h * 160, 160)])
+                lambda h: sblk.at[pl.ds(h * 160, 160)], pause=True)
     pull(sgen)
+    local[3].wait()
+    for d in range(3):
+        links.recv(first + 7 + d, dslot(ysrc[d + 1]), ydev[3 - d])
+    dgen = ring(links, NZ, z, zdev[1], zdev[7], lambda t, h: dbuf.at[t, pl.ds(h * 256, 256)],
+                lambda h: dshard.at[pl.ds(h * 256, 256)])
+    dkeep = pltpu.make_async_copy(dshard, dbuf.at[z], ls.at[3])
+    dkeep.start()
+    pull(dgen)
     while pull(lgen):
         pass
     for k, d in ((0, 0), (2, 1), (4, 3), (6, 2)):
@@ -204,6 +226,8 @@
         links.recv(sibs + k + 1, dcols.at[t, :, 1 - c, b], sib)
     local[0].wait()
 
+    for _ in range(4):
+        pull(dgen)
     acc[...] = jnp.zeros_like(acc)
 
     @pl.loop(0, 8)
@@ -220,14 +244,16 @@
     for d in range(3):
         links.send(base + d, ush.at[column_slice(y + d + 1, z)], ubuf.at[z, kblock(y)], ydev[d + 1])
     own.start()
+    for _ in range(4):
+        pull(dgen)
+    pull(sgen)
     own.wait()
     for d in range(3):
         links.recv(base + d, ubuf.at[z, kblock(ysrc[d + 1])], ydev[3 - d])
     ugen = ring(links, NZ, z, zdev[1], zdev[7], lambda t, h: ubuf.at[t, pl.ds(h * 512, 512)])
     pull(ugen)
-    local[3].wait()
-    for d in range(3):
-        links.recv(first + 7 + d, dslot(ysrc[d + 1]), ydev[3 - d])
+    for _ in range(2):
+        pull(dgen)
 
     pair, xs, zs = links.slot(5), links.slot(15), links.slot(8)
     slab = lambda k: zbuf.at[pl.ds(k * 5, 5)]
@@ -287,9 +313,12 @@
             for d in sorted({k, NZ - k}):
                 links.send(zs + d, fin.at[(z + d) % NZ], slab(z), zdev[d])
 
-    pull(sgen)
-    pull(sgen)
-    for _ in range(4):
+    for _ in range(2):
+        pull(sgen)
+        pull(ugen)
+        pull(ugen)
+    for _ in range(2):
+        pull(ugen)
         pull(ugen)
     while pull(sgen):
         pass
@@ -297,8 +326,6 @@
     multiply(0)
     multiply(1)
     across(0)
-    for _ in range(4):
-        pull(ugen)
     multiply(2)
     across(1)
     onward(0)
@@ -314,13 +341,6 @@
     across(4)
     onward(3)
     onward(4)
-    dgen = ring(links, NZ, z, zdev[1], zdev[7], lambda t, h: dbuf.at[t, pl.ds(h * 256, 256)],
-                lambda h: dshard.at[pl.ds(h * 256, 256)])
-    dkeep = pltpu.make_async_copy(dshard, dbuf.at[z], ls.at[0])
-    dkeep.start()
-    pull(dgen)
-    for _ in range(4):
-        pull(dgen)
     zkeep.wait()
     for d in (1, 7, 2, 6, 3, 5, 4):
         links.recv(zs + d, slab((z + 8 - d) % NZ), zdev[8 - d])
@@ -332,12 +352,17 @@
     spot = lambda yy, gg: rows.at[:, gg, :, pl.ds(pl.multiple_of(column_slice(yy, z) * 128, 128), 128)]
     for t, q in plane:
         links.send(ps + 8 * t + q, snd.at[(g + q) % 8], spot(y, g), peer(t, q))
-    home = pltpu.make_async_copy(snd.at[g], spot(y, g), ls.at[3])
+    home = pltpu.make_async_copy(snd.at[g], spot(y, g), ls.at[0])
     home.start()
     while pull(dgen):
         pass
+    dkeep.wait()
+    over_rows = (((0,), (0,)), ((), ()))
+    drows = dcols[:, x, c].reshape(512, 512)
+    for k in range(8):
+        fpd[k] = lax.dot_general(dbuf[k], drows, over_rows, preferred_element_type=jnp.float32)
+        utr[k] = jnp.transpose(ubuf[k])
     home.wait()
-    dkeep.wait()
     for t, q in plane:
         links.recv(ps + 8 * t + q, spot((y + 4 - t) % 4, (g + 8 - q) % 8), peer(4 - t, 8 - q))
     sig[...] = rows[y].reshape(256, 512)
@@ -358,14 +383,9 @@
             src_ref=got.at[q], dst_ref=got.at[q], send_sem=ss.at[fs + q], recv_sem=rs.at[fs + q],
             device_id=(src(q), z), device_id_type=MESH)
 
-    drows = dcols[:, x, c].reshape(512, 512)
     srows = rows[...].reshape(1024, 512)
-    over_rows = (((0,), (0,)), ((), ()))
     for k in range(8):
-        fp[k] = (
-            lax.dot_general(dbuf[k], drows, over_rows, preferred_element_type=jnp.float32)
-            - lax.dot_general(ubuf[k], srows, over_rows, preferred_element_type=jnp.float32)
-        ).astype(BF)
+        fp[k] = (fpd[k] - jnp.dot(utr[k], srows, preferred_element_type=jnp.float32)).astype(BF)
 
         @pl.when(dest(k) != r)
         def _():
@@ -390,15 +410,14 @@
 
 
 def per_device(sigma_anc, lower_off, inverse_diag, structure):
-    blocks = sigma_anc.reshape(5, 8, 40, 256)
-    ssel = jnp.take(blocks, structure, axis=2).reshape(5, 8, 4, 8, 256)
-    ssel = jnp.transpose(ssel, (3, 2, 0, 1, 4)).reshape(8, 160, 256)
-    dsh = jnp.transpose(inverse_diag.reshape(128, 4, 128), (1, 0, 2))
+    ssel = pl.pallas_call(
+        choose, out_shape=jax.ShapeDtypeStruct((8, 160, 256), BF), in_specs=[VM, SM], out_specs=VM,
+        name="choose_columns")(sigma_anc, structure)
     nsem = 210
     return pl.pallas_call(
         mega,
         out_shape=(jax.ShapeDtypeStruct((256, 512), BF), jax.ShapeDtypeStruct((128, 512), jnp.float32)),
-        in_specs=[ANY] * 4 + [SM], out_specs=[VM, VM],
+        in_specs=[ANY, ANY, ANY, SM], out_specs=[VM, VM],
         scratch_shapes=[
             pltpu.SemaphoreType.DMA((nsem,)), pltpu.SemaphoreType.DMA((nsem,)), pltpu.SemaphoreType.DMA((4,)),
             pltpu.VMEM((8, 256, 512), BF), pltpu.VMEM((4, 4, 2, 128, 512), BF), pltpu.VMEM((512, 128), BF),
@@ -408,10 +427,11 @@
             pltpu.VMEM((5, 4, 2, 160, 256), BF), pltpu.VMEM((5, 4, 160, 256), BF),
             pltpu.VMEM((5, 4, 160, 256), BF), pltpu.VMEM((5, 3, 160, 256), BF),
             pltpu.VMEM((8, 5, 32, 128), BF), pltpu.VMEM((40, 32, 128), BF), pltpu.VMEM((8, 4, 32, 128), BF),
-            pltpu.VMEM((4, 8, 32, 512), BF), pltpu.VMEM((8, 128, 512), BF), pltpu.VMEM((8, 128, 512), BF)],
+            pltpu.VMEM((4, 8, 32, 512), BF), pltpu.VMEM((8, 128, 512), BF), pltpu.VMEM((8, 128, 512), BF),
+            pltpu.VMEM((8, 128, 512), jnp.float32), pltpu.VMEM((8, 128, 1024), BF)],
         compiler_params=pltpu.CompilerParams(
             collective_id=1, has_side_effects=True, vmem_limit_bytes=60 * 2**20),
-        name="selected_inverse")(lower_off, inverse_diag, dsh, ssel, structure)
+        name="selected_inverse")(lower_off, inverse_diag, ssel, structure)
 
 
 def solution(mesh):

time: 145 us -> 136 us (0.938)
  Pallas kernels: 136 us -> 132 us
  local copies, waits for them, and re-layouts: 6.31 us -> 2.42 us
    pallas_call x1, Pallas kernels: 136 us -> 130 us  [per_device(): pl.pallas_call(mega, out_shape=(jax.ShapeDtypeStruct((256, 512), BF), jax...]
    pallas_call x0 -> x1, Pallas kernels: none -> 2.09 us  [per_device(): pl.pallas_call(choose, out_shape=jax.ShapeDtypeStruct((8, 160, 256), BF),...]
    unnamed x11 -> x4, local copies, waits for them, and re-layouts: 3.61 us -> 2.42 us
where the time goes in v3:
time: 136 us; the launch traced here: 135 us
  Pallas kernels  132 us (97%)
  local copies, waits for them, and re-layouts  2.42 us (2%)
    pallas_call x1, Pallas kernels, per_device(): pl.pallas_call(mega, out_shape=(jax.ShapeDtypeStruct((256, 512), BF), jax...  130 us

profile of v3, /device:TPU:24, one launch (start us, length us, event | category | flops | bytes accessed | tf_op | source)
XLA Modules:
  0.0 134.7 jit_solution(7739896217048596487)
XLA Ops:
  0.6 2.1 %choose_columns.1.ssel = bf16[8,160,256]{2,1,0:T(8,128)(2,1)} custom-call(bf16[5,8,10240]{2,1,0:T(8,128)(2,1)} %anc.1, s32[32]{0:T(128)} %structure.3), custom_call_target="tpu_custom_call" | custom-call | tf_op jit(solution)/shard_map/choose_columns/pallas_call | solution.py:413
  2.7 129.5 %selected_inverse.1 = (bf16[256,512]{1,0:T(8,128)(2,1)}, f32[128,512]{1,0:T(8,128)}) custom-call(bf16[256,512]{1,0:T(8,128)(2,1)} %low.1, bf16[128,512]{1,0:T(8,128)(2,1)} %diag.1, bf16[8,160,256]{2,1,0:T(8,128)(2,1)} %choose_columns.1.ssel, s32[32]{0:T(128)} %structure.3), custom_call_target="tpu_custom_call" | custom-call | tf_op jit(solution)/shard_map/selected_inverse/pallas_call | solution.py:417
  132.3 0.0 copy-start
  132.3 1.7 %copy.8 = bf16[256,512]{1,0:T(8,128)(2,1)} copy(bf16[256,512]{1,0:T(8,128)(2,1)} %get-tuple-element.4) | data formatting | bytes 524288
  134.0 0.0 copy-done
  134.0 0.7 copy.9
Async XLA Ops:
  132.3 1.7 %copy-start = (f32[128,512]{1,0:T(8,128)S(1)}, f32[128,512]{1,0:T(8,128)}, u32[]{:S(2)}) copy-start(f32[128,512]{1,0:T(8,128)} %get-tuple-element.5) | copy-start | bytes 786436

commit v4 on v3

--- a/solution.py
+++ b/solution.py
@@ -61,29 +61,28 @@
             cp.wait_send()
 
 
-def ring(links, n, me, nxt, prv, view, own=None, pause=False):
-    steps = n // 2
-    base = links.slot(4 * steps)
+def ring(links, n, me, nxt, prv, view, own=None, pieces=2, pause=False):
+    steps, half = n // 2, pieces // 2
+    base = links.slot(2 * pieces * steps)
     own = own or (lambda h: view(me, h))
-    idx = lambda d, s, h: base + (d * steps + s) * 2 + h
+    idx = lambda d, s, h: base + (d * steps + s) * pieces + h
     for s in range(steps):
-        for pos in range(1 if s == steps - 1 else 2):
-            if pause and s == 0 and pos == 1:
+        for pos in range(half if s == steps - 1 else pieces):
+            if pause and s == 0 and pos == half:
                 yield
-            for d, h in ((0, pos), (1, 1 - pos)):
+            for d, h in ((0, pos), (1, pieces - 1 - pos)):
                 shard = lax.rem(me + (n - s if d == 0 else s), n)
                 if s:
                     yield
                     links.recv(idx(d, s - 1, h), view(shard, h), prv if d == 0 else nxt)
                 src = own(h) if s == 0 else view(shard, h)
                 links.send(idx(d, s, h), src, view(shard, h), nxt if d == 0 else prv)
-    yield
-    for s, pos in ((steps - 2, 1), (steps - 1, 0)):
-        for d, h in ((0, pos), (1, 1 - pos)):
-            shard = lax.rem(me + (n - s - 1 if d == 0 else s + 1), n)
-            links.recv(idx(d, s, h), view(shard, h), prv if d == 0 else nxt)
-        if pos:
-            yield
+    for s, first in ((steps - 2, half), (steps - 1, 0)):
+        yield
+        for pos in range(first, first + half):
+            for d, h in ((0, pos), (1, pieces - 1 - pos)):
+                shard = lax.rem(me + (n - s - 1 if d == 0 else s + 1), n)
+                links.recv(idx(d, s, h), view(shard, h), prv if d == 0 else nxt)
 
 
 def pull(gen):
@@ -92,6 +91,11 @@
         return True
     except StopIteration:
         return False
+
+
+def pulls(gen, count):
+    for _ in range(count):
+        pull(gen)
 
 
 def run(*gens):
@@ -116,7 +120,7 @@
 def mega(low, diag, ssel, structure, sig, front, ss, rs, ls,
 
          strip, dcols, dshard, s1, sblk, sfull, acc, ush, ubuf, dbuf,
-         part, pbuf, abuf, xbuf, fin, zbuf, snd, rows, fp, got, fpd, utr):
+         part, pbuf, abuf, xbuf, fin, zbuf, snd, rows, fp, fpair, fsum, got, fpd, utr):
     y, x, c, z = coords()
     g = x * 2 + c
     r = y * 8 + g
@@ -130,7 +134,7 @@
     peer = lambda t, q: (((y + t) % NY) * 8 + (g + q) % 8, z)
     greet([zdev[1], zdev[7]] + [peer(0, q) for q in range(1, 8)] + ydev[1:])
 
-    a, b = pl.ds(0, 64), pl.ds(64, 64)
+    a, b = pl.ds(0, 96), pl.ds(96, 32)
     dslot = lambda t: dshard.at[pl.ds(pl.multiple_of(t * 128, 128), 128)]
     dsl = lambda t: diag.at[:, pl.ds(pl.multiple_of(column_slice(t, z) * 128, 128), 128)]
     local = [
@@ -139,28 +143,27 @@
         pltpu.make_async_copy(ssel.at[g], s1.at[g], ls.at[2]),
         pltpu.make_async_copy(dsl(y), dslot(y), ls.at[3]),
     ]
-    lgen = ring(links, NZ, z, zdev[1], zdev[7], lambda t, h: strip.at[t, pl.ds(h * 128, 128)],
-                lambda h: low.at[pl.ds(h * 128, 128)])
+    lgen = ring(links, NZ, z, zdev[1], zdev[7], lambda t, h: strip.at[t, pl.ds(h * 64, 64)],
+                lambda h: low.at[pl.ds(h * 64, 64)], 4)
     pull(lgen)
-    a1 = ring(links, NY, y, ydev[1], ydev[3], lambda t, h: dcols.at[t, x, c, pl.ds(h * 32, 32)],
-              lambda h: diag.at[pl.ds(h * 32, 32)])
-    b1 = ring(links, NX, x, xdev[1], xdev[3], lambda t, h: dcols.at[y, t, c, pl.ds(64 + h * 32, 32)],
-              lambda h: diag.at[pl.ds(64 + h * 32, 32)])
+    a1 = ring(links, NY, y, ydev[1], ydev[3], lambda t, h: dcols.at[t, x, c, pl.ds(h * 48, 48)],
+              lambda h: diag.at[pl.ds(h * 48, 48)])
+    b1 = ring(links, NX, x, xdev[1], xdev[3], lambda t, h: dcols.at[y, t, c, pl.ds(96 + h * 16, 16)],
+              lambda h: diag.at[pl.ds(96 + h * 16, 16)])
     pull(a1)
     pull(b1)
-    for cp in (local[1], local[0], local[3]):
+    first = links.slot(10)
+    for d in (3, 2, 4, 1, 5, 0, 6):
+        q = (g + d + 1) % 8
+        links.send(first + d, ssel.at[q], s1.at[g], dev(y, q // 2, q % 2, z))
+    for cp in (local[1], local[0], local[2], local[3]):
         cp.start()
-    local[2].start()
     run(a1, b1)
     local[1].wait()
     a2 = ring(links, NX, x, xdev[1], xdev[3], lambda t, h: dcols.at[pl.ds(2 * h, 2), t, c, a])
     b2 = ring(links, NY, y, ydev[1], ydev[3], lambda t, h: dcols.at[t, pl.ds(2 * h, 2), c, b])
     pull(a2)
     pull(b2)
-    first = links.slot(10)
-    for d in (3, 2, 4, 1, 5, 0, 6):
-        q = (g + d + 1) % 8
-        links.send(first + d, ssel.at[q], s1.at[g], dev(y, q // 2, q % 2, z))
     for d in range(3):
         links.send(first + 7 + d, dsl(y + d + 1), dslot(y), ydev[d + 1])
     sibs = links.slot(8)
@@ -172,23 +175,7 @@
         links.send(sibs + k + 1, dcols.at[t, :, c, b], dcols.at[t, :, c, b], sib)
 
     share(0, 0)
-    for _ in range(2):
-        pull(lgen)
-        pull(lgen)
-        pull(a2)
-        pull(b2)
-    for _ in range(2):
-        pull(lgen)
-        pull(lgen)
-    pull(a2)
-    pull(b2)
-    share(2, 1)
-    share(4, 3)
-    for _ in range(2):
-        pull(lgen)
-    pull(a2)
-    pull(b2)
-    share(6, 2)
+    pulls(lgen, 8)
 
     local[2].wait()
     for d in range(7):
@@ -209,6 +196,18 @@
     sgen = ring(links, NY, y, ydev[1], ydev[3], lambda t, h: sfull.at[t, pl.ds(h * 160, 160)],
                 lambda h: sblk.at[pl.ds(h * 160, 160)], pause=True)
     pull(sgen)
+    for _ in range(2):
+        pulls(lgen, 4)
+        pull(a2)
+        pull(b2)
+    pull(a2)
+    pull(b2)
+    share(2, 1)
+    share(4, 3)
+    pulls(lgen, 4)
+    pull(a2)
+    pull(b2)
+    share(6, 2)
     local[3].wait()
     for d in range(3):
         links.recv(first + 7 + d, dslot(ysrc[d + 1]), ydev[3 - d])
@@ -226,8 +225,6 @@
         links.recv(sibs + k + 1, dcols.at[t, :, 1 - c, b], sib)
     local[0].wait()
 
-    for _ in range(4):
-        pull(dgen)
     acc[...] = jnp.zeros_like(acc)
 
     @pl.loop(0, 8)
@@ -244,16 +241,13 @@
     for d in range(3):
         links.send(base + d, ush.at[column_slice(y + d + 1, z)], ubuf.at[z, kblock(y)], ydev[d + 1])
     own.start()
-    for _ in range(4):
-        pull(dgen)
     pull(sgen)
     own.wait()
     for d in range(3):
         links.recv(base + d, ubuf.at[z, kblock(ysrc[d + 1])], ydev[3 - d])
-    ugen = ring(links, NZ, z, zdev[1], zdev[7], lambda t, h: ubuf.at[t, pl.ds(h * 512, 512)])
+    ugen = ring(links, NZ, z, zdev[1], zdev[7], lambda t, h: ubuf.at[t, pl.ds(h * 256, 256)], pieces=4)
     pull(ugen)
-    for _ in range(2):
-        pull(dgen)
+    pulls(sgen, 2)
 
     pair, xs, zs = links.slot(5), links.slot(15), links.slot(8)
     slab = lambda k: zbuf.at[pl.ds(k * 5, 5)]
@@ -303,7 +297,7 @@
             total = abuf[k, x, at, :n].astype(jnp.float32)
             for d in range(3):
                 total = total + xbuf[k, d, at, :n].astype(jnp.float32)
-            total = (-total).astype(BF)
+            total = total.astype(BF)
             for m, t in enumerate(ids):
                 fin[t, j] = total[:, m * 128:(m + 1) * 128]
 
@@ -313,24 +307,18 @@
             for d in sorted({k, NZ - k}):
                 links.send(zs + d, fin.at[(z + d) % NZ], slab(z), zdev[d])
 
-    for _ in range(2):
-        pull(sgen)
-        pull(ugen)
-        pull(ugen)
-    for _ in range(2):
-        pull(ugen)
-        pull(ugen)
+    pulls(ugen, 8)
     while pull(sgen):
         pass
     keep.wait()
     multiply(0)
     multiply(1)
     across(0)
+    pulls(ugen, 8)
     multiply(2)
     across(1)
     onward(0)
-    for _ in range(3):
-        pull(ugen)
+    pulls(ugen, 5)
     multiply(3)
     across(2)
     onward(1)
@@ -360,52 +348,67 @@
     over_rows = (((0,), (0,)), ((), ()))
     drows = dcols[:, x, c].reshape(512, 512)
     for k in range(8):
-        fpd[k] = lax.dot_general(dbuf[k], drows, over_rows, preferred_element_type=jnp.float32)
-        utr[k] = jnp.transpose(ubuf[k])
+        at = pl.ds((k % 2) * 128, 128)
+        fpd[k // 2, at] = lax.dot_general(dbuf[k], drows, over_rows, preferred_element_type=jnp.float32)
+        utr[k // 2, at] = jnp.transpose(ubuf[k])
     home.wait()
     for t, q in plane:
         links.recv(ps + 8 * t + q, spot((y + 4 - t) % 4, (g + 8 - q) % 8), peer(4 - t, 8 - q))
     sig[...] = rows[y].reshape(256, 512)
 
-    fs = links.slot(8)
+    srows = rows[...].reshape(1024, 512)
+    cores, over_x = links.slot(2), links.slot(8)
+
+    def product(k):
+        return fpd[k] + jnp.dot(utr[k], srows, preferred_element_type=jnp.float32)
+
+    for m in range(2):
+        k = 2 * m + (y + 1 - c) % 2
+        fp[m] = product(k).astype(BF)
+        links.send(cores + m, fp.at[m], fpair.at[m], sib)
+
+    def outgoing(m, e):
+        k = 2 * m + (y + c) % 2
+        j = (y + k) % 4
+        to = (k * 8 + (2 * e + j // 2) * 2 + c, z)
+        return to[0] != r, pltpu.make_async_remote_copy(
+            src_ref=fsum.at[m, pl.ds(e * 128, 128)], dst_ref=got.at[x], send_sem=ss.at[over_x + 2 * m + e],
+            recv_sem=rs.at[over_x + x], device_id=to, device_id_type=MESH)
+
     from_y = (r % 4 + 4 - y) % 4
-    is_self = from_y == y
-    dest = lambda k: 4 * k + column_slice(y, k)
-    src = lambda q: from_y * 8 + q
-
-    def outgoing(k):
-        return pltpu.make_async_remote_copy(
-            src_ref=fp.at[k], dst_ref=got.at[g], send_sem=ss.at[fs + k], recv_sem=rs.at[fs + g],
-            device_id=(dest(k), z), device_id_type=MESH)
-
-    def incoming(q):
-        return pltpu.make_async_remote_copy(
-            src_ref=got.at[q], dst_ref=got.at[q], send_sem=ss.at[fs + q], recv_sem=rs.at[fs + q],
-            device_id=(src(q), z), device_id_type=MESH)
-
-    srows = rows[...].reshape(1024, 512)
-    for k in range(8):
-        fp[k] = (fpd[k] - jnp.dot(utr[k], srows, preferred_element_type=jnp.float32)).astype(BF)
-
-        @pl.when(dest(k) != r)
+
+    for m in range(2):
+        k = 2 * m + (y + c) % 2
+        total = product(k)
+        links.recv(cores + m, fpair.at[m], sib)
+        fsum[m] = (total + fpair[m].astype(jnp.float32)).astype(BF)
+        for e in range(2):
+            away, cp = outgoing(m, e)
+
+            @pl.when(away)
+            def _():
+                cp.start()
+
+            @pl.when(jnp.logical_not(away))
+            def _():
+                got[x] = fsum[m, e * 128:(e + 1) * 128]
+
+    front[...] = jnp.zeros_like(front)
+    for q in range(4):
+        frm = from_y * 8 + q * 2 + c
+
+        @pl.when(frm != r)
         def _():
-            outgoing(k).start()
-
-    @pl.when(is_self)
-    def _():
-        got[g] = fp[r // 4]
-
-    front[...] = jnp.zeros_like(front)
-    for q in range(8):
-        @pl.when(src(q) != r)
-        def _():
-            incoming(q).wait_recv()
+            links.recv(over_x + q, got.at[q], (frm, z))
 
         front[...] += got[q].astype(jnp.float32)
-    for k in range(8):
-        @pl.when(dest(k) != r)
-        def _():
-            outgoing(k).wait_send()
+    for m in range(2):
+        for e in range(2):
+            away, cp = outgoing(m, e)
+
+            @pl.when(away)
+            def _():
+                cp.wait_send()
     links.drain()
 
 
@@ -413,8 +416,8 @@
     ssel = pl.pallas_call(
         choose, out_shape=jax.ShapeDtypeStruct((8, 160, 256), BF), in_specs=[VM, SM], out_specs=VM,
         name="choose_columns")(sigma_anc, structure)
-    nsem = 210
-    return pl.pallas_call(
+    nsem = 256
+    negated, front = pl.pallas_call(
         mega,
         out_shape=(jax.ShapeDtypeStruct((256, 512), BF), jax.ShapeDtypeStruct((128, 512), jnp.float32)),
         in_specs=[ANY, ANY, ANY, SM], out_specs=[VM, VM],
@@ -427,11 +430,13 @@
             pltpu.VMEM((5, 4, 2, 160, 256), BF), pltpu.VMEM((5, 4, 160, 256), BF),
             pltpu.VMEM((5, 4, 160, 256), BF), pltpu.VMEM((5, 3, 160, 256), BF),
             pltpu.VMEM((8, 5, 32, 128), BF), pltpu.VMEM((40, 32, 128), BF), pltpu.VMEM((8, 4, 32, 128), BF),
-            pltpu.VMEM((4, 8, 32, 512), BF), pltpu.VMEM((8, 128, 512), BF), pltpu.VMEM((8, 128, 512), BF),
-            pltpu.VMEM((8, 128, 512), jnp.float32), pltpu.VMEM((8, 128, 1024), BF)],
+            pltpu.VMEM((4, 8, 32, 512), BF), pltpu.VMEM((2, 256, 512), BF), pltpu.VMEM((2, 256, 512), BF),
+            pltpu.VMEM((2, 256, 512), BF), pltpu.VMEM((4, 128, 512), BF),
+            pltpu.VMEM((4, 256, 512), jnp.float32), pltpu.VMEM((4, 256, 1024), BF)],
         compiler_params=pltpu.CompilerParams(
             collective_id=1, has_side_effects=True, vmem_limit_bytes=60 * 2**20),
         name="selected_inverse")(lower_off, inverse_diag, ssel, structure)
+    return -negated, front
 
 
 def solution(mesh):

time: 136 us -> 128 us (0.941)
  Pallas kernels: 132 us -> 123 us
  other arithmetic: 0 us -> 1.74 us
  local copies, waits for them, and re-layouts: 2.42 us -> 0.71 us
    pallas_call x1, Pallas kernels: 130 us -> 121 us  [per_device(): pl.pallas_call(mega, out_shape=(jax.ShapeDtypeStruct((256, 512), BF), jax...]
    neg x0 -> x1, other arithmetic: none -> 1.74 us  [per_device(): return (-negated, front)]
    unnamed x4 -> x3, local copies, waits for them, and re-layouts: 2.42 us -> 0.71 us
where the time goes in v4:
time: 128 us; the launch traced here: 126 us
  Pallas kernels  123 us (96%)
  other arithmetic  1.74 us (1%)
    pallas_call x1, Pallas kernels, per_device(): pl.pallas_call(mega, out_shape=(jax.ShapeDtypeStruct((256, 512), BF), jax...  121 us

profile of v4, /device:TPU:24, one launch (start us, length us, event | category | flops | bytes accessed | tf_op | source)
XLA Modules:
  0.0 126.1 jit_solution(13857241702247179628)
XLA Ops:
  0.6 2.1 %choose_columns.1.ssel = bf16[8,160,256]{2,1,0:T(8,128)(2,1)} custom-call(bf16[5,8,10240]{2,1,0:T(8,128)(2,1)} %anc.1, s32[32]{0:T(128)} %structure.3), custom_call_target="tpu_custom_call" | custom-call | tf_op jit(solution)/shard_map/choose_columns/pallas_call | solution.py:416
  2.7 120.9 %selected_inverse.1 = (bf16[256,512]{1,0:T(8,128)(2,1)}, f32[128,512]{1,0:T(8,128)}) custom-call(bf16[256,512]{1,0:T(8,128)(2,1)} %low.1, bf16[128,512]{1,0:T(8,128)(2,1)} %diag.1, bf16[8,160,256]{2,1,0:T(8,128)(2,1)} %choose_columns.1.ssel, s32[32]{0:T(128)} %structure.3), custom_call_target="tpu_custom_call" | custom-call | tf_op jit(solution)/shard_map/selected_inverse/pallas_call | solution.py:420
  123.7 0.0 copy-start
  123.7 1.7 %neg.3 = bf16[256,512]{1,0:T(8,128)(2,1)} negate(bf16[256,512]{1,0:T(8,128)(2,1)} %get-tuple-element.4) | non-fusion elementwise | flops 131072 | bytes 524288 | tf_op jit(solution)/shard_map/neg | solution.py:439
  125.4 0.0 copy-done
  125.4 0.7 copy.7
Async XLA Ops:
  123.7 1.8 %copy-start = (f32[128,512]{1,0:T(8,128)S(1)}, f32[128,512]{1,0:T(8,128)}, u32[]{:S(2)}) copy-start(f32[128,512]{1,0:T(8,128)} %get-tuple-element.9) | copy-start | bytes 786436

commit v5 on v4

--- a/solution.py
+++ b/solution.py
@@ -204,6 +204,7 @@
     pull(b2)
     share(2, 1)
     share(4, 3)
+    pull(sgen)
     pulls(lgen, 4)
     pull(a2)
     pull(b2)
@@ -241,7 +242,6 @@
     for d in range(3):
         links.send(base + d, ush.at[column_slice(y + d + 1, z)], ubuf.at[z, kblock(y)], ydev[d + 1])
     own.start()
-    pull(sgen)
     own.wait()
     for d in range(3):
         links.recv(base + d, ubuf.at[z, kblock(ysrc[d + 1])], ydev[3 - d])
@@ -312,9 +312,10 @@
         pass
     keep.wait()
     multiply(0)
+    pulls(ugen, 4)
     multiply(1)
     across(0)
-    pulls(ugen, 8)
+    pulls(ugen, 4)
     multiply(2)
     across(1)
     onward(0)
@@ -337,9 +338,10 @@
     for q in range(8):
         for t in range(4):
             snd[q, t] = zbuf[structure[8 * t + q]]
-    spot = lambda yy, gg: rows.at[:, gg, :, pl.ds(pl.multiple_of(column_slice(yy, z) * 128, 128), 128)]
-    for t, q in plane:
-        links.send(ps + 8 * t + q, snd.at[(g + q) % 8], spot(y, g), peer(t, q))
+    spot = lambda yy, gg: rows.at[column_slice(yy, z), :, gg]
+    for t in (0, 1, 3, 2):
+        for q in range(1 if t == 0 else 0, 8):
+            links.send(ps + 8 * t + q, snd.at[(g + q) % 8], spot(y, g), peer(t, q))
     home = pltpu.make_async_copy(snd.at[g], spot(y, g), ls.at[0])
     home.start()
     while pull(dgen):
@@ -349,66 +351,84 @@
     drows = dcols[:, x, c].reshape(512, 512)
     for k in range(8):
         at = pl.ds((k % 2) * 128, 128)
-        fpd[k // 2, at] = lax.dot_general(dbuf[k], drows, over_rows, preferred_element_type=jnp.float32)
+        both = lax.dot_general(dbuf[k], drows, over_rows, preferred_element_type=jnp.float32)
+        for j in range(4):
+            fpd[j, k // 2, at] = both[:, j * 128:(j + 1) * 128]
         utr[k // 2, at] = jnp.transpose(ubuf[k])
     home.wait()
-    for t, q in plane:
-        links.recv(ps + 8 * t + q, spot((y + 4 - t) % 4, (g + 8 - q) % 8), peer(4 - t, 8 - q))
-    sig[...] = rows[y].reshape(256, 512)
-
-    srows = rows[...].reshape(1024, 512)
-    cores, over_x = links.slot(2), links.slot(8)
-
-    def product(k):
-        return fpd[k] + jnp.dot(utr[k], srows, preferred_element_type=jnp.float32)
-
-    for m in range(2):
-        k = 2 * m + (y + 1 - c) % 2
-        fp[m] = product(k).astype(BF)
-        links.send(cores + m, fp.at[m], fpair.at[m], sib)
-
-    def outgoing(m, e):
-        k = 2 * m + (y + c) % 2
-        j = (y + k) % 4
-        to = (k * 8 + (2 * e + j // 2) * 2 + c, z)
+
+    cores, over_x = links.slot(4), links.slot(16)
+    from_y = (r % 4 + 4 - y) % 4
+    theirs, ours = (y + 1 - c) % 2, (y + c) % 2
+
+    def product(t, m, kind):
+        k = 2 * m + kind
+        slot = column_slice((y + 4 - t) % 4, z)
+        right = rows[slot].reshape(1024, 128)
+        return fpd[slot, k] + jnp.dot(utr[k], right, preferred_element_type=jnp.float32)
+
+    def start_slice(t):
+        for q in range(1 if t == 0 else 0, 8):
+            links.recv(ps + 8 * t + q, spot((y + 4 - t) % 4, (g + 8 - q) % 8), peer(4 - t, 8 - q))
+        for m in range(2):
+            fp[t, m] = product(t, m, theirs).astype(BF)
+        links.send(cores + t, fp.at[t], fpair.at[t], sib)
+
+    def outgoing(t, m, e):
+        k = 2 * m + ours
+        to = (k * 8 + (2 * e + (y + k) % 4 // 2) * 2 + c, z)
+        i = over_x + 4 * t
         return to[0] != r, pltpu.make_async_remote_copy(
-            src_ref=fsum.at[m, pl.ds(e * 128, 128)], dst_ref=got.at[x], send_sem=ss.at[over_x + 2 * m + e],
-            recv_sem=rs.at[over_x + x], device_id=to, device_id_type=MESH)
-
-    from_y = (r % 4 + 4 - y) % 4
-
-    for m in range(2):
-        k = 2 * m + (y + c) % 2
-        total = product(k)
-        links.recv(cores + m, fpair.at[m], sib)
-        fsum[m] = (total + fpair[m].astype(jnp.float32)).astype(BF)
-        for e in range(2):
-            away, cp = outgoing(m, e)
-
-            @pl.when(away)
+            src_ref=fsum.at[t, m, pl.ds(e * 128, 128)], dst_ref=got.at[column_slice((y + 4 - t) % 4, z), x],
+            send_sem=ss.at[i + 2 * m + e], recv_sem=rs.at[i + x], device_id=to, device_id_type=MESH)
+
+    def finish_slice(t):
+        for m in range(2):
+            total = product(t, m, ours)
+            if m == 0:
+                links.recv(cores + t, fpair.at[t], sib)
+            fsum[t, m] = (total + fpair[t, m].astype(jnp.float32)).astype(BF)
+            for e in range(2):
+                away, cp = outgoing(t, m, e)
+
+                @pl.when(away)
+                def _():
+                    cp.start()
+
+                @pl.when(jnp.logical_not(away))
+                def _():
+                    got[column_slice((y + 4 - t) % 4, z), x] = fsum[t, m, e * 128:(e + 1) * 128]
+
+    turns = (0, 1, 3, 2)
+    start_slice(turns[0])
+    for before, t in zip(turns, turns[1:]):
+        finish_slice(before)
+        start_slice(t)
+    finish_slice(turns[-1])
+    for j in range(4):
+        sig[:, j * 128:(j + 1) * 128] = rows[j, y].reshape(256, 128)
+
+    for t in turns:
+        slot = column_slice((from_y + 4 - t) % 4, z)
+        for q in range(4):
+            frm = from_y * 8 + q * 2 + c
+
+            @pl.when(frm != r)
             def _():
-                cp.start()
-
-            @pl.when(jnp.logical_not(away))
-            def _():
-                got[x] = fsum[m, e * 128:(e + 1) * 128]
-
-    front[...] = jnp.zeros_like(front)
-    for q in range(4):
-        frm = from_y * 8 + q * 2 + c
-
-        @pl.when(frm != r)
-        def _():
-            links.recv(over_x + q, got.at[q], (frm, z))
-
-        front[...] += got[q].astype(jnp.float32)
-    for m in range(2):
-        for e in range(2):
-            away, cp = outgoing(m, e)
-
-            @pl.when(away)
-            def _():
-                cp.wait_send()
+                links.recv(over_x + 4 * t + q, got.at[slot, q], (frm, z))
+    for j in range(4):
+        total = got[j, 0].astype(jnp.float32)
+        for q in range(1, 4):
+            total = total + got[j, q].astype(jnp.float32)
+        front[:, j * 128:(j + 1) * 128] = total
+    for t in turns:
+        for m in range(2):
+            for e in range(2):
+                away, cp = outgoing(t, m, e)
+
+                @pl.when(away)
+                def _():
+                    cp.wait_send()
     links.drain()
 
 
@@ -416,7 +436,7 @@
     ssel = pl.pallas_call(
         choose, out_shape=jax.ShapeDtypeStruct((8, 160, 256), BF), in_specs=[VM, SM], out_specs=VM,
         name="choose_columns")(sigma_anc, structure)
-    nsem = 256
+    nsem = 272
     negated, front = pl.pallas_call(
         mega,
         out_shape=(jax.ShapeDtypeStruct((256, 512), BF), jax.ShapeDtypeStruct((128, 512), jnp.float32)),
@@ -430,9 +450,9 @@
             pltpu.VMEM((5, 4, 2, 160, 256), BF), pltpu.VMEM((5, 4, 160, 256), BF),
             pltpu.VMEM((5, 4, 160, 256), BF), pltpu.VMEM((5, 3, 160, 256), BF),
             pltpu.VMEM((8, 5, 32, 128), BF), pltpu.VMEM((40, 32, 128), BF), pltpu.VMEM((8, 4, 32, 128), BF),
-            pltpu.VMEM((4, 8, 32, 512), BF), pltpu.VMEM((2, 256, 512), BF), pltpu.VMEM((2, 256, 512), BF),
-            pltpu.VMEM((2, 256, 512), BF), pltpu.VMEM((4, 128, 512), BF),
-            pltpu.VMEM((4, 256, 512), jnp.float32), pltpu.VMEM((4, 256, 1024), BF)],
+            pltpu.VMEM((4, 4, 8, 32, 128), BF), pltpu.VMEM((4, 2, 256, 128), BF), pltpu.VMEM((4, 2, 256, 128), BF),
+            pltpu.VMEM((4, 2, 256, 128), BF), pltpu.VMEM((4, 4, 128, 128), BF),
+            pltpu.VMEM((4, 4, 256, 128), jnp.float32), pltpu.VMEM((4, 256, 1024), BF)],
         compiler_params=pltpu.CompilerParams(
             collective_id=1, has_side_effects=True, vmem_limit_bytes=60 * 2**20),
         name="selected_inverse")(lower_off, inverse_diag, ssel, structure)

time: 128 us -> 120 us (0.938)
  Pallas kernels: 123 us -> 116 us
    pallas_call x1, Pallas kernels: 121 us -> 114 us  [per_device(): pl.pallas_call(mega, out_shape=(jax.ShapeDtypeStruct((256, 512), BF), jax...]
where the time goes in v5:
time: 120 us; the launch traced here: 119 us
  Pallas kernels  116 us (97%)
  other arithmetic  1.74 us (1%)
    pallas_call x1, Pallas kernels, per_device(): pl.pallas_call(mega, out_shape=(jax.ShapeDtypeStruct((256, 512), BF), jax...  114 us

profile of v5, /device:TPU:24, one launch (start us, length us, event | category | flops | bytes accessed | tf_op | source)
XLA Modules:
  0.0 119.1 jit_solution(10991299919383988242)
XLA Ops:
  0.6 2.1 %choose_columns.1.ssel = bf16[8,160,256]{2,1,0:T(8,128)(2,1)} custom-call(bf16[5,8,10240]{2,1,0:T(8,128)(2,1)} %anc.1, s32[32]{0:T(128)} %structure.3), custom_call_target="tpu_custom_call" | custom-call | tf_op jit(solution)/shard_map/choose_columns/pallas_call | solution.py:436
  2.7 113.9 %selected_inverse.1 = (bf16[256,512]{1,0:T(8,128)(2,1)}, f32[128,512]{1,0:T(8,128)}) custom-call(bf16[256,512]{1,0:T(8,128)(2,1)} %low.1, bf16[128,512]{1,0:T(8,128)(2,1)} %diag.1, bf16[8,160,256]{2,1,0:T(8,128)(2,1)} %choose_columns.1.ssel, s32[32]{0:T(128)} %structure.3), custom_call_target="tpu_custom_call" | custom-call | tf_op jit(solution)/shard_map/selected_inverse/pallas_call | solution.py:440
  116.6 0.0 copy-start
  116.6 1.7 %neg.3 = bf16[256,512]{1,0:T(8,128)(2,1)} negate(bf16[256,512]{1,0:T(8,128)(2,1)} %get-tuple-element.4) | non-fusion elementwise | flops 131072 | bytes 524288 | tf_op jit(solution)/shard_map/neg | solution.py:459
  118.4 0.0 copy-done
  118.4 0.7 copy.7
Async XLA Ops:
  116.6 1.8 %copy-start = (f32[128,512]{1,0:T(8,128)S(1)}, f32[128,512]{1,0:T(8,128)}, u32[]{:S(2)}) copy-start(f32[128,512]{1,0:T(8,128)} %get-tuple-element.9) | copy-start | bytes 786436

commit v6 on v5

--- a/solution.py
+++ b/solution.py
@@ -26,13 +26,6 @@
 
 def dev(y, x, c, z):
     return ((y * NX + x) * NC + c, z)
-
-
-def greet(peers):
-    sem = pltpu.get_barrier_semaphore()
-    for peer in peers:
-        pl.semaphore_signal(sem, inc=1, device_id=peer, device_id_type=MESH)
-    pl.semaphore_wait(sem, len(peers))
 
 
 class Links:
@@ -108,16 +101,12 @@
                 live.remove(g)
 
 
-def choose(anc, structure, ssel):
-    for q in range(8):
-        picked = []
-        for t in range(4):
-            at = pl.ds(pl.multiple_of(structure[8 * t + q] * 256, 256), 256)
-            picked.append(anc[:, :, at].astype(jnp.float32).reshape(40, 256))
-        ssel[q] = jnp.concatenate(picked, axis=0).astype(BF)
-
-
-def mega(low, diag, ssel, structure, sig, front, ss, rs, ls,
+def finish(negated, total, sig, front):
+    sig[...] = -negated[...]
+    front[...] = total[...]
+
+
+def mega(low, diag, anc, structure, sig, front, ss, rs, ls, ancb, ssel,
 
          strip, dcols, dshard, s1, sblk, sfull, acc, ush, ubuf, dbuf,
          part, pbuf, abuf, xbuf, fin, zbuf, snd, rows, fp, fpair, fsum, got, fpd, utr):
@@ -132,7 +121,16 @@
     sib = dev(y, x, 1 - c, z)
     plane = [(t, q) for t in range(4) for q in range(8)][1:]
     peer = lambda t, q: (((y + t) % NY) * 8 + (g + q) % 8, z)
-    greet([zdev[1], zdev[7]] + [peer(0, q) for q in range(1, 8)] + ydev[1:])
+    near_by = [zdev[1], zdev[7]] + [peer(0, q) for q in range(1, 8)] + ydev[1:]
+    entry = pltpu.get_barrier_semaphore()
+    for other in near_by:
+        pl.semaphore_signal(entry, inc=1, device_id=other, device_id_type=MESH)
+    for k in range(40):
+        ancb[k] = anc[:, :, k * 256:(k + 1) * 256].astype(jnp.float32)
+    for q in range(8):
+        picked = [ancb[structure[8 * t + q]].reshape(40, 256) for t in range(4)]
+        ssel[q] = jnp.concatenate(picked, axis=0).astype(BF)
+    pl.semaphore_wait(entry, len(near_by))
 
     a, b = pl.ds(0, 96), pl.ds(96, 32)
     dslot = lambda t: dshard.at[pl.ds(pl.multiple_of(t * 128, 128), 128)]
@@ -433,16 +431,14 @@
 
 
 def per_device(sigma_anc, lower_off, inverse_diag, structure):
-    ssel = pl.pallas_call(
-        choose, out_shape=jax.ShapeDtypeStruct((8, 160, 256), BF), in_specs=[VM, SM], out_specs=VM,
-        name="choose_columns")(sigma_anc, structure)
     nsem = 272
     negated, front = pl.pallas_call(
         mega,
         out_shape=(jax.ShapeDtypeStruct((256, 512), BF), jax.ShapeDtypeStruct((128, 512), jnp.float32)),
-        in_specs=[ANY, ANY, ANY, SM], out_specs=[VM, VM],
+        in_specs=[ANY, ANY, VM, SM], out_specs=[VM, VM],
         scratch_shapes=[
             pltpu.SemaphoreType.DMA((nsem,)), pltpu.SemaphoreType.DMA((nsem,)), pltpu.SemaphoreType.DMA((4,)),
+            pltpu.VMEM((40, 5, 8, 256), jnp.float32), pltpu.VMEM((8, 160, 256), BF),
             pltpu.VMEM((8, 256, 512), BF), pltpu.VMEM((4, 4, 2, 128, 512), BF), pltpu.VMEM((512, 128), BF),
             pltpu.VMEM((8, 160, 256), BF), pltpu.VMEM((320, 1024), BF), pltpu.VMEM((4, 320, 1024), BF),
             pltpu.VMEM((256, 512), jnp.float32), pltpu.VMEM((4, 256, 128), BF), pltpu.VMEM((8, 1024, 128), BF),
@@ -455,8 +451,11 @@
             pltpu.VMEM((4, 4, 256, 128), jnp.float32), pltpu.VMEM((4, 256, 1024), BF)],
         compiler_params=pltpu.CompilerParams(
             collective_id=1, has_side_effects=True, vmem_limit_bytes=60 * 2**20),
-        name="selected_inverse")(lower_off, inverse_diag, ssel, structure)
-    return -negated, front
+        name="selected_inverse")(lower_off, inverse_diag, sigma_anc, structure)
+    return pl.pallas_call(
+        finish,
+        out_shape=(jax.ShapeDtypeStruct((256, 512), BF), jax.ShapeDtypeStruct((128, 512), jnp.float32)),
+        in_specs=[VM, VM], out_specs=[VM, VM], name="finish")(negated, front)
 
 
 def solution(mesh):

time: 120 us -> 118 us (0.983)
  other arithmetic: 1.74 us -> 0 us
    neg x1 -> x0, other arithmetic: 1.74 us -> none  [per_device(): return (-negated, front)]
where the time goes in v6:
time: 118 us; the launch traced here: 117 us
  Pallas kernels  116 us (98%)
    pallas_call x1, Pallas kernels, per_device(): pl.pallas_call(mega, out_shape=(jax.ShapeDtypeStruct((256, 512), BF), jax...  115 us

profile of v6, /device:TPU:24, one launch (start us, length us, event | category | flops | bytes accessed | tf_op | source)
XLA Modules:
  0.0 117.0 jit_solution(2839166671215109484)
XLA Ops:
  0.6 114.5 %selected_inverse.1 = (bf16[256,512]{1,0:T(8,128)(2,1)}, f32[128,512]{1,0:T(8,128)}) custom-call(bf16[256,512]{1,0:T(8,128)(2,1)} %low.1, bf16[128,512]{1,0:T(8,128)(2,1)} %diag.1, bf16[5,8,10240]{2,1,0:T(8,128)(2,1)} %anc.1, s32[32]{0:T(128)} %structure.1), custom_call_target="tpu_custom_call" | custom-call | tf_op jit(solution)/shard_map/selected_inverse/pallas_call | solution.py:435
  115.2 1.8 %finish.1 = (bf16[256,512]{1,0:T(8,128)(2,1)}, f32[128,512]{1,0:T(8,128)}) custom-call(bf16[256,512]{1,0:T(8,128)(2,1)} %get-tuple-element.4.negated, f32[128,512]{1,0:T(8,128)} %get-tuple-element.5.total), custom_call_target="tpu_custom_call" | custom-call | tf_op jit(solution)/shard_map/finish/pallas_call | solution.py:455

commit v7 on v6

--- a/solution.py
+++ b/solution.py
@@ -328,6 +328,9 @@
     across(4)
     onward(3)
     onward(4)
+    for k in range(8):
+        utr[k // 2, (k % 2) * 128:(k % 2 + 1) * 128] = jnp.transpose(ubuf[k])
+    pulls(dgen, 4)
     zkeep.wait()
     for d in (1, 7, 2, 6, 3, 5, 4):
         links.recv(zs + d, slab((z + 8 - d) % NZ), zdev[8 - d])
@@ -352,7 +355,6 @@
         both = lax.dot_general(dbuf[k], drows, over_rows, preferred_element_type=jnp.float32)
         for j in range(4):
             fpd[j, k // 2, at] = both[:, j * 128:(j + 1) * 128]
-        utr[k // 2, at] = jnp.transpose(ubuf[k])
     home.wait()
 
     cores, over_x = links.slot(4), links.slot(16)

time: 118 us -> 117 us (level)
  no operation moved by 1% of the time
where the time goes in v7:
time: 117 us; the launch traced here: 116 us
  Pallas kernels  115 us (98%)
    pallas_call x1, Pallas kernels, per_device(): pl.pallas_call(mega, out_shape=(jax.ShapeDtypeStruct((256, 512), BF), jax...  113 us

profile of v7, /device:TPU:24, one launch (start us, length us, event | category | flops | bytes accessed | tf_op | source)
XLA Modules:
  0.0 115.9 jit_solution(2716597137745707707)
XLA Ops:
  0.6 113.4 %selected_inverse.1 = (bf16[256,512]{1,0:T(8,128)(2,1)}, f32[128,512]{1,0:T(8,128)}) custom-call(bf16[256,512]{1,0:T(8,128)(2,1)} %low.1, bf16[128,512]{1,0:T(8,128)(2,1)} %diag.1, bf16[5,8,10240]{2,1,0:T(8,128)(2,1)} %anc.1, s32[32]{0:T(128)} %structure.1), custom_call_target="tpu_custom_call" | custom-call | tf_op jit(solution)/shard_map/selected_inverse/pallas_call | solution.py:437
  114.1 1.8 %finish.1 = (bf16[256,512]{1,0:T(8,128)(2,1)}, f32[128,512]{1,0:T(8,128)}) custom-call(bf16[256,512]{1,0:T(8,128)(2,1)} %get-tuple-element.4.negated, f32[128,512]{1,0:T(8,128)} %get-tuple-element.5.total), custom_call_target="tpu_custom_call" | custom-call | tf_op jit(solution)/shard_map/finish/pallas_call | solution.py:457

commit v8 on v7

--- a/solution.py
+++ b/solution.py
@@ -125,14 +125,6 @@
     entry = pltpu.get_barrier_semaphore()
     for other in near_by:
         pl.semaphore_signal(entry, inc=1, device_id=other, device_id_type=MESH)
-    for k in range(40):
-        ancb[k] = anc[:, :, k * 256:(k + 1) * 256].astype(jnp.float32)
-    for q in range(8):
-        picked = [ancb[structure[8 * t + q]].reshape(40, 256) for t in range(4)]
-        ssel[q] = jnp.concatenate(picked, axis=0).astype(BF)
-    pl.semaphore_wait(entry, len(near_by))
-
-    a, b = pl.ds(0, 96), pl.ds(96, 32)
     dslot = lambda t: dshard.at[pl.ds(pl.multiple_of(t * 128, 128), 128)]
     dsl = lambda t: diag.at[:, pl.ds(pl.multiple_of(column_slice(t, z) * 128, 128), 128)]
     local = [
@@ -141,23 +133,31 @@
         pltpu.make_async_copy(ssel.at[g], s1.at[g], ls.at[2]),
         pltpu.make_async_copy(dsl(y), dslot(y), ls.at[3]),
     ]
+    for k in (0, 1, 3):
+        local[k].start()
+    for k in range(40):
+        ancb[k] = anc[:, :, k * 256:(k + 1) * 256].astype(jnp.float32)
+    for q in range(8):
+        picked = [ancb[structure[8 * t + q]].reshape(40, 256) for t in range(4)]
+        ssel[q] = jnp.concatenate(picked, axis=0).astype(BF)
+    local[2].start()
+    pl.semaphore_wait(entry, len(near_by))
+    local[0].wait()
+    local[1].wait()
+
+    a, b = pl.ds(0, 96), pl.ds(96, 32)
     lgen = ring(links, NZ, z, zdev[1], zdev[7], lambda t, h: strip.at[t, pl.ds(h * 64, 64)],
-                lambda h: low.at[pl.ds(h * 64, 64)], 4)
+                pieces=4)
     pull(lgen)
-    a1 = ring(links, NY, y, ydev[1], ydev[3], lambda t, h: dcols.at[t, x, c, pl.ds(h * 48, 48)],
-              lambda h: diag.at[pl.ds(h * 48, 48)])
-    b1 = ring(links, NX, x, xdev[1], xdev[3], lambda t, h: dcols.at[y, t, c, pl.ds(96 + h * 16, 16)],
-              lambda h: diag.at[pl.ds(96 + h * 16, 16)])
+    a1 = ring(links, NY, y, ydev[1], ydev[3], lambda t, h: dcols.at[t, x, c, pl.ds(h * 48, 48)])
+    b1 = ring(links, NX, x, xdev[1], xdev[3], lambda t, h: dcols.at[y, t, c, pl.ds(96 + h * 16, 16)])
     pull(a1)
     pull(b1)
     first = links.slot(10)
     for d in (3, 2, 4, 1, 5, 0, 6):
         q = (g + d + 1) % 8
         links.send(first + d, ssel.at[q], s1.at[g], dev(y, q // 2, q % 2, z))
-    for cp in (local[1], local[0], local[2], local[3]):
-        cp.start()
     run(a1, b1)
-    local[1].wait()
     a2 = ring(links, NX, x, xdev[1], xdev[3], lambda t, h: dcols.at[pl.ds(2 * h, 2), t, c, a])
     b2 = ring(links, NY, y, ydev[1], ydev[3], lambda t, h: dcols.at[t, pl.ds(2 * h, 2), c, b])
     pull(a2)
@@ -222,7 +222,6 @@
         links.recv(sibs + k, dcols.at[:, t, 1 - c, a], sib)
         t = ysrc[d]
         links.recv(sibs + k + 1, dcols.at[t, :, 1 - c, b], sib)
-    local[0].wait()
 
     acc[...] = jnp.zeros_like(acc)
 

time: 117 us -> 117 us (level)
  no operation moved by 1% of the time
where the time goes in v8:
time: 117 us; the launch traced here: 116 us
  Pallas kernels  115 us (98%)
    pallas_call x1, Pallas kernels, per_device(): pl.pallas_call(mega, out_shape=(jax.ShapeDtypeStruct((256, 512), BF), jax...  113 us

profile of v8, /device:TPU:24, one launch (start us, length us, event | category | flops | bytes accessed | tf_op | source)
XLA Modules:
  0.0 115.8 jit_solution(2900196069594763804)
XLA Ops:
  0.6 113.3 %selected_inverse.1 = (bf16[256,512]{1,0:T(8,128)(2,1)}, f32[128,512]{1,0:T(8,128)}) custom-call(bf16[256,512]{1,0:T(8,128)(2,1)} %low.1, bf16[128,512]{1,0:T(8,128)(2,1)} %diag.1, bf16[5,8,10240]{2,1,0:T(8,128)(2,1)} %anc.1, s32[32]{0:T(128)} %structure.1), custom_call_target="tpu_custom_call" | custom-call | tf_op jit(solution)/shard_map/selected_inverse/pallas_call | solution.py:436
  113.9 1.8 %finish.1 = (bf16[256,512]{1,0:T(8,128)(2,1)}, f32[128,512]{1,0:T(8,128)}) custom-call(bf16[256,512]{1,0:T(8,128)(2,1)} %get-tuple-element.4.negated, f32[128,512]{1,0:T(8,128)} %get-tuple-element.5.total), custom_call_target="tpu_custom_call" | custom-call | tf_op jit(solution)/shard_map/finish/pallas_call | solution.py:456
